TPU v7x, 32 devices: a whole 2x2x4 slice. The times are simulated.
32 devices in a mesh: fsdp: 4 (over z), own: 8 (over y, x, core).
Axes of the slice: x: 2, y: 2, z: 4, core: 2. Of those that a mesh axis runs over, the one named last changes fastest.
Arguments:
- activations: bfloat16 [8192, 8192], P('own', 'fsdp'), may hold values from -6 to 6
- cotangent: bfloat16 [8192, 2048], P('own', 'fsdp'), may hold values from -6 to 6
- frozen_weight: bfloat16 [8192, 2048], P('fsdp', 'own'), may hold values from -0.0625 to 0.0625
- down_weight: bfloat16 [32, 8192, 128], P('own', 'fsdp'), may hold values from -0.0625 to 0.0625
- up_weight: bfloat16 [32, 64, 2048], P('own', None, 'fsdp'), may hold values from -0.1875 to 0.1875
- slot_of_adapter: int32 [32], replicated, may hold values from 0 to 31, as said below
- tenant_of_block: int32 [64], replicated, may hold values from 0 to 31, as said below
Outputs:
- activation_gradient: bfloat16 [8192, 8192], P('own', 'fsdp')
- down_gradient: bfloat16 [32, 8192, 128], P('own', 'fsdp')
- up_gradient: bfloat16 [32, 64, 2048], P('own', None, 'fsdp')
Inputs may be any that keep to these rules, and one draw needn't show every extreme that they name: A permutation of the slots: the adapter t is held in row slot_of_adapter[t] of down_weight and up_weight, which lies on own index slot_of_adapter[t] // 4. `tenant_of_block`: bin b holds blocks b * 8 to (b + 1) * 8 - 1. Within a bin the blocks of one adapter stand in one run, and two blocks whose adapters lie on the same own index have the same adapter.
All inputs are finite; a program needn't handle non-finite values.
Results may differ from a plain program's by a relative error of at most 0.0057.
Values may be sent and summed in bfloat16 or wider, within the bound.
A program may use at most 128 MiB of HBM per device.

v0:
```python
import jax
import jax.numpy as jnp
from jax import lax
from jax.sharding import PartitionSpec as P

KEY_VALUE_WIDTH = 1024
BLOCK = 128


def select_rows(table, stacked):
    flat = stacked.reshape(stacked.shape[0], -1)
    picked = jnp.dot(table, flat, preferred_element_type=jnp.bfloat16)
    return picked.reshape((table.shape[0],) + stacked.shape[1:])


def shards(
    activations, cotangent, frozen_weight, down_weight, up_weight, slot_of_adapter, tenant_of_block
):
    own_count = lax.axis_size("own")
    own_index = lax.axis_index("own")
    fsdp_index = lax.axis_index("fsdp")
    tok_rows = activations.shape[0]
    width_part = activations.shape[1]
    col_count = cotangent.shape[1]
    resident_count = down_weight.shape[0]
    paired_rank = down_weight.shape[2]
    rank_half = paired_rank // 2
    block_count = tok_rows // BLOCK
    slot_table = slot_of_adapter[tenant_of_block].reshape(own_count, block_count)
    owner_table = slot_table // resident_count
    local_table = slot_table % resident_count
    wanted_mask = owner_table == own_index
    wanted_any = jnp.any(wanted_mask, axis=1)
    wanted_local = jnp.max(jnp.where(wanted_mask, local_table, 0), axis=1)
    held_ids = jnp.arange(resident_count, dtype=jnp.int32)
    service_table = ((wanted_local[:, None] == held_ids[None, :]) & wanted_any[:, None]).astype(
        jnp.bfloat16
    )
    outgoing_down = select_rows(service_table, down_weight)
    outgoing_up = select_rows(service_table, up_weight)
    fetched_a, fetched_b = (
        lax.all_to_all(outgoing_down, "own", split_axis=0, concat_axis=0, tiled=True),
        lax.all_to_all(outgoing_up, "own", split_axis=0, concat_axis=0, tiled=True),
    )
    my_owner = lax.dynamic_index_in_dim(owner_table, own_index, 0, keepdims=False)
    owner_ids = jnp.arange(own_count, dtype=jnp.int32)
    block_pick = (my_owner[:, None] == owner_ids[None, :]).astype(jnp.bfloat16)
    block_a = select_rows(block_pick, fetched_a)
    block_b = select_rows(block_pick, fetched_b)
    x_blocks = activations.reshape(block_count, BLOCK, width_part)
    g_blocks = cotangent.reshape(block_count, BLOCK, col_count)
    inner_part = jnp.einsum(
        "btd,bdr->btr", x_blocks, block_a, preferred_element_type=jnp.float32
    ).reshape(tok_rows, paired_rank)
    proj_index = fsdp_index * col_count // KEY_VALUE_WIDTH
    q_single = jnp.einsum(
        "btc,brc->btr", g_blocks, block_b, preferred_element_type=jnp.float32
    ).reshape(tok_rows, rank_half)
    is_value = proj_index.astype(jnp.float32)
    q_part = jnp.concatenate([q_single * (1.0 - is_value), q_single * is_value], axis=1)
    inner_sum, q_sum = lax.psum((inner_part, q_part), "fsdp")
    inner_low = inner_sum.astype(jnp.bfloat16)
    q_low = q_sum.astype(jnp.bfloat16)
    inner_mine = lax.dynamic_slice_in_dim(inner_low, proj_index * rank_half, rank_half, 1)
    part_b = jnp.einsum(
        "btr,btc->brc",
        inner_mine.reshape(block_count, BLOCK, rank_half),
        g_blocks,
        preferred_element_type=jnp.float32,
    )
    q_blocks = q_low.reshape(block_count, BLOCK, paired_rank)
    part_a = jnp.einsum("btd,btr->bdr", x_blocks, q_blocks, preferred_element_type=jnp.float32)
    same_owner = (my_owner[:, None] == my_owner[None, :]).astype(jnp.float32)
    merged_a = jnp.einsum(
        "jk,kdr->jdr", same_owner, part_a, precision=lax.Precision.HIGHEST
    ).astype(jnp.bfloat16)
    merged_b = jnp.einsum(
        "jk,kdr->jdr", same_owner, part_b, precision=lax.Precision.HIGHEST
    ).astype(jnp.bfloat16)
    leading = jnp.concatenate([jnp.ones((1,), jnp.bool_), my_owner[1:] != my_owner[:-1]])
    route_table = ((owner_ids[:, None] == my_owner[None, :]) & leading[None, :]).astype(
        jnp.bfloat16
    )
    send_grad_a = select_rows(route_table, merged_a)
    send_grad_b = select_rows(route_table, merged_b)
    back_a, back_b = (
        lax.all_to_all(send_grad_a, "own", split_axis=0, concat_axis=0, tiled=True),
        lax.all_to_all(send_grad_b, "own", split_axis=0, concat_axis=0, tiled=True),
    )
    serve_cols = service_table.T
    down_gradient = jnp.dot(
        serve_cols, back_a.reshape(own_count, -1), preferred_element_type=jnp.float32
    )
    down_gradient = down_gradient.astype(jnp.bfloat16).reshape(down_weight.shape)
    up_gradient = jnp.dot(
        serve_cols, back_b.reshape(own_count, -1), preferred_element_type=jnp.float32
    )
    up_gradient = up_gradient.astype(jnp.bfloat16).reshape(up_weight.shape)
    weight_rows = lax.all_gather(frozen_weight, "own", axis=1, tiled=True)
    full_grad = lax.all_gather(cotangent, "fsdp", axis=1, tiled=True)
    frozen_gradient = lax.dot_general(
        full_grad, weight_rows, (((1,), (1,)), ((), ())), preferred_element_type=jnp.float32
    )
    adapter_gradient = jnp.einsum(
        "mch,myh->mcy", q_blocks, block_a, preferred_element_type=jnp.float32
    ).reshape(tok_rows, width_part)
    activation_gradient = (frozen_gradient + adapter_gradient).astype(jnp.bfloat16)
    return (activation_gradient, down_gradient, up_gradient)


def solution(mesh):
    return jax.shard_map(
        shards,
        mesh=mesh,
        in_specs=(
            P("own", "fsdp"),
            P("own", "fsdp"),
            P("fsdp", "own"),
            P("own", "fsdp", None),
            P("own", None, "fsdp"),
            P(),
            P(),
        ),
        out_specs=(P("own", "fsdp"), P("own", "fsdp", None), P("own", None, "fsdp")),
        check_vma=False,
    )
```

profile of v0, /device:TPU:0, one launch (start us, length us, event | category | flops | bytes accessed | tf_op | source)
XLA Modules:
  0.0 250.4 jit_solution(8154095647235994908)
XLA Ops:
  7.2 0.0 copy-start
  7.2 0.0 copy-start.5
  7.2 0.0 all-gather.3.cloned.1.call-start
  7.2 0.7 all-gather.3.cloned.1.call-update
  7.9 0.0 all-gather.5.cloned.1.call-start
  8.0 0.7 all-gather.5.cloned.1.call-update
  8.7 0.7 compare_select_fusion
  9.3 0.0 copy-done
  9.4 0.8 gather_fusion
  10.1 0.1 reshape.82
  10.2 0.1 fusion.57
  10.3 0.1 fusion.26
  10.5 1.3 fusion.53
  11.8 0.9 copy.30
  12.7 5.2 %all-to-all-start = ((bf16[8,64,512]{2,1,0:T(8,128)(2,1)}), bf16[8,64,512]{2,1,0:T(8,128)(2,1)S(1)}, u32[]{:S(2)}, u32[]{:S(2)}) async-start(bf16[8,64,512]{2,1,0:T(8,128)(2,1)} %copy.30), calls=%async_computation | async-start | bytes 1048576 | tf_op jit(solution)/shard_map/all_to_all | solution.py:43
  17.9 0.0 copy-done.5
  17.9 10.0 %fusion.12 = bf16[8,2048,128]{2,0,1:T(8,128)(2,1)S(1)} fusion(bf16[1,4,2048,128]{3,2,1,0:T(8,128)(2,1)S(1)} %bitcast.134, pred[8,4]{0,1:T(4,128)(4,1)S(1)} %fusion.51), kind=kOutput, calls=%fused_computation.20 | convolution fusion | flops 16777216 | bytes 6291488 | tf_op jit(solution)/shard_map/dot_general | solution.py:12
  27.9 2.7 %copy.35 = bf16[8,2048,128]{2,1,0:T(8,128)(2,1)} copy(bf16[8,2048,128]{2,0,1:T(8,128)(2,1)S(1)} %fusion.12) | data formatting | bytes 8388608 | tf_op jit(solution)/shard_map/dot_general | solution.py:12
  30.6 0.0 copy-start.4
  30.6 0.0 all-to-all-done
  30.6 4.9 %all-to-all-start.1 = ((bf16[8,2048,128]{2,1,0:T(8,128)(2,1)}), bf16[8,2048,128]{2,1,0:T(8,128)(2,1)}, u32[]{:S(2)}, u32[]{:S(2)}) async-start(bf16[8,2048,128]{2,1,0:T(8,128)(2,1)} %copy.35), calls=%async_computation.1 | async-start | bytes 8388608 | tf_op jit(solution)/shard_map/all_to_all | solution.py:42
  35.6 0.1 compare_bitcast_fusion
  35.6 0.1 pad_add_fusion
  35.7 0.4 fusion.30
  36.2 0.0 copy-done.4
  36.2 0.5 multiply_bitcast_fusion.1
  36.8 47.8 %all-to-all-done.1 = bf16[8,2048,128]{2,1,0:T(8,128)(2,1)} async-done(((bf16[8,2048,128]{2,1,0:T(8,128)(2,1)}), bf16[8,2048,128]{2,1,0:T(8,128)(2,1)}, u32[]{:S(2)}, u32[]{:S(2)}) %all-to-all-start.1) | async-done | bytes 4194336 | tf_op jit(solution)/shard_map/all_to_all | solution.py:42
  84.6 0.0 copy-start.3
  84.6 4.9 %fusion.3 = bf16[8,2048,128]{2,0,1:T(8,128)(2,1)S(1)} fusion(bf16[1,8,2048,128]{3,2,1,0:T(8,128)(2,1)} %bitcast.50, s32[8]{0:T(128)S(1)} %fusion.77), kind=kOutput, calls=%fused_computation.9 | convolution fusion | flops 33554496 | bytes 8388640 | tf_op jit(solution)/shard_map/dot_general | solution.py:12
  89.5 0.0 copy-start.2
  89.5 0.0 copy-done.3
  89.5 1.8 fusion.8
  91.3 0.2 copy-done.2
  91.5 0.2 copy.41
  91.7 42.1 %all-reduce.2 = (bf16[1024,128]{0,1:T(8,128)(2,1)S(1)}, bf16[1024,128]{0,1:T(8,128)(2,1)S(1)}) all-reduce(f32[1024,128]{0,1:T(8,128)S(1)} %pad_maximum_fusion, f32[1024,128]{0,1:T(8,128)S(1)} %copy.41), channel_id=1, replica_groups=mesh['fsdp'=4,'own'=8] {'fsdp'}, use_global_device_ids=true, to_apply=%region_2.3 | all-reduce | flops 262144 | bytes 1572864 | tf_op jit(solution)/shard_map/psum | solution.py:61
  133.7 0.2 copy.34
  133.9 0.3 fusion.22
  134.2 1.2 fusion.17
  135.4 0.3 fusion.39
  135.7 0.9 copy.44
  136.6 3.8 %all-to-all-start.3 = ((bf16[8,64,512]{2,1,0:T(8,128)(2,1)}), bf16[8,64,512]{2,1,0:T(8,128)(2,1)S(1)}, u32[]{:S(2)}, u32[]{:S(2)}) async-start(bf16[8,64,512]{2,1,0:T(8,128)(2,1)} %copy.44), calls=%async_computation.3 | async-start | bytes 1048576 | tf_op jit(solution)/shard_map/all_to_all | solution.py:88
  140.5 6.7 %convolution_bitcast_fusion = f32[8,2048,128]{1,2,0:T(8,128)} fusion(bf16[8,128,128]{2,1,0:T(8,128)(2,1)S(1)} %bitcast.132, bf16[8,128,2048]{2,1,0:T(8,128)(2,1)} %bitcast.128), kind=kOutput, calls=%fused_computation.5 | convolution fusion | flops 536870912 | bytes 12845056 | tf_op jit(solution)/shard_map/btd,btr->bdr/dot_general | solution.py:72
  147.2 9.4 %copy.38 = f32[8,2048,128]{2,0,1:T(8,128)} copy(f32[8,2048,128]{1,2,0:T(8,128)} %convolution_bitcast_fusion) | data formatting | bytes 16777216 | tf_op jit(solution)/shard_map/btd,btr->bdr/dot_general | solution.py:72
  156.5 7.5 %fusion.35 = bf16[8,2048,128]{2,0,1:T(8,128)(2,1)S(1)} fusion(f32[8,2048,128]{2,0,1:T(8,128)} %copy.38, s32[8]{0:T(128)S(1)} %fusion.77), kind=kOutput, calls=%fused_computation.56 | convolution fusion | flops 201326656 | bytes 12582944 | tf_op jit(solution)/shard_map/jk,kdr->jdr/dot_general | solution.py:74
  164.1 1.2 fusion.5
  165.3 2.6 %copy.39 = bf16[8,2048,128]{2,1,0:T(8,128)(2,1)} copy(bf16[8,2048,128]{2,0,1:T(8,128)(2,1)S(1)} %fusion.5) | data formatting | bytes 8388608 | tf_op jit(solution)/shard_map/dot_general | solution.py:12
  167.9 0.0 all-to-all-done.3
  168.0 4.8 %all-to-all-start.2 = ((bf16[8,2048,128]{2,1,0:T(8,128)(2,1)}), bf16[8,2048,128]{2,1,0:T(8,128)(2,1)}, u32[]{:S(2)}, u32[]{:S(2)}) async-start(bf16[8,2048,128]{2,1,0:T(8,128)(2,1)} %copy.39), calls=%async_computation.2 | async-start | bytes 8388608 | tf_op jit(solution)/shard_map/all_to_all | solution.py:87
  172.8 6.7 %fusion.10 = f32[8,128,2048]{2,1,0:T(8,128)} fusion(bf16[8,128,128]{2,1,0:T(8,128)(2,1)S(1)} %bitcast.133, bf16[8,2048,128]{2,0,1:T(8,128)(2,1)} %copy-done.2), kind=kOutput, calls=%fused_computation.16 | convolution fusion | flops 536870912 | bytes 12845056 | tf_op jit(solution)/shard_map/mch,myh->mcy/dot_general | solution.py:104
  179.5 0.3 copy.55
  179.8 0.3 convolution_convert_fusion.1
  180.1 0.7 copy.98
  180.8 41.1 %all-to-all-done.2 = bf16[8,2048,128]{2,1,0:T(8,128)(2,1)} async-done(((bf16[8,2048,128]{2,1,0:T(8,128)(2,1)}), bf16[8,2048,128]{2,1,0:T(8,128)(2,1)}, u32[]{:S(2)}, u32[]{:S(2)}) %all-to-all-start.2) | async-done | bytes 4194336 | tf_op jit(solution)/shard_map/all_to_all | solution.py:87
  221.9 4.9 %fusion.14 = bf16[1,4,2048,128]{3,1,2,0:T(4,128)(2,1)S(1)} fusion(pred[8,4]{0,1:T(4,128)(4,1)S(1)} %fusion.51, bf16[1,8,2048,128]{3,2,1,0:T(8,128)(2,1)} %bitcast.52), kind=kOutput, calls=%fused_computation.22 | convolution fusion | flops 17825792 | bytes 6291488 | tf_op jit(solution)/shard_map/dot_general | solution.py:91
  226.8 1.6 copy.97
  228.4 0.0 all-gather.3.cloned.1.call-done
  228.4 0.0 all-gather.5.cloned.1.call-done
  228.4 0.0 copy-start.1
  228.4 15.1 %fusion = bf16[1024,2048]{1,0:T(8,128)(2,1)} fusion(f32[8,128,2048]{2,1,0:T(8,128)} %fusion.10, bf16[1024,2048]{1,0:T(8,128)(2,1)} %all-gather.3.cloned.1.call-done, bf16[2048,2048]{1,0:T(8,128)(2,1)} %all-gather.5.cloned.1.call-done), kind=kOutput, calls=%fused_computation.4 | convolution fusion | flops 8594128896 | bytes 25165824 | tf_op jit(solution)/shard_map/dot_general | solution.py:101
  243.5 0.0 copy-done.1
  (6 shorter events, 0.1 us)
Async XLA Ops:
  7.2 2.2 copy-start
  7.2 10.7 %copy-start.5 = (bf16[4,2048,128]{2,1,0:T(8,128)(2,1)S(1)}, bf16[4,2048,128]{2,1,0:T(8,128)(2,1)}, u32[]{:S(2)}) copy-start(bf16[4,2048,128]{2,1,0:T(8,128)(2,1)} %param.10) | copy-start | bytes 6291460
  7.2 221.2 %all-gather.3.cloned.1.call-start = ((), (), s32[]{:S(2)}) async-start(), calls=%async_computation.4 | async-start | bytes 5242880 | tf_op jit(solution)/shard_map/all_gather | solution.py:100
  7.9 220.5 %all-gather.5.cloned.1.call-start = ((), (), s32[]{:S(2)}) async-start(), calls=%async_computation.5 | async-start | bytes 9437184 | tf_op jit(solution)/shard_map/all_gather | solution.py:99
  12.7 17.9 %all-to-all-start = ((bf16[8,64,512]{2,1,0:T(8,128)(2,1)}), bf16[8,64,512]{2,1,0:T(8,128)(2,1)S(1)}, u32[]{:S(2)}, u32[]{:S(2)}) async-start(bf16[8,64,512]{2,1,0:T(8,128)(2,1)} %copy.30), calls=%async_computation | async-start | bytes 1048576 | tf_op jit(solution)/shard_map/all_to_all | solution.py:43
  30.6 5.6 %copy-start.4 = (bf16[1024,512]{1,0:T(8,128)(2,1)S(1)}, bf16[1024,512]{1,0:T(8,128)(2,1)}, u32[]{:S(2)}) copy-start(bf16[1024,512]{1,0:T(8,128)(2,1)} %param.8) | copy-start | bytes 3145732
  30.6 54.0 %all-to-all-start.1 = ((bf16[8,2048,128]{2,1,0:T(8,128)(2,1)}), bf16[8,2048,128]{2,1,0:T(8,128)(2,1)}, u32[]{:S(2)}, u32[]{:S(2)}) async-start(bf16[8,2048,128]{2,1,0:T(8,128)(2,1)} %copy.35), calls=%async_computation.1 | async-start | bytes 8388608 | tf_op jit(solution)/shard_map/all_to_all | solution.py:42
  84.6 4.9 %copy-start.3 = (bf16[1024,2048]{1,0:T(8,128)(2,1)S(1)}, bf16[1024,2048]{1,0:T(8,128)(2,1)}, u32[]{:S(2)}) copy-start(bf16[1024,2048]{1,0:T(8,128)(2,1)} %param.7) | copy-start | bytes 12582916
  89.5 2.0 copy-start.2
  136.6 31.3 %all-to-all-start.3 = ((bf16[8,64,512]{2,1,0:T(8,128)(2,1)}), bf16[8,64,512]{2,1,0:T(8,128)(2,1)S(1)}, u32[]{:S(2)}, u32[]{:S(2)}) async-start(bf16[8,64,512]{2,1,0:T(8,128)(2,1)} %copy.44), calls=%async_computation.3 | async-start | bytes 1048576 | tf_op jit(solution)/shard_map/all_to_all | solution.py:88
  168.0 53.9 %all-to-all-start.2 = ((bf16[8,2048,128]{2,1,0:T(8,128)(2,1)}), bf16[8,2048,128]{2,1,0:T(8,128)(2,1)}, u32[]{:S(2)}, u32[]{:S(2)}) async-start(bf16[8,2048,128]{2,1,0:T(8,128)(2,1)} %copy.39), calls=%async_computation.2 | async-start | bytes 8388608 | tf_op jit(solution)/shard_map/all_to_all | solution.py:87
  228.4 15.1 %copy-start.1 = (s32[32]{0:T(128)S(1)}, s32[32]{0:T(128)}, u32[]{:S(2)}) copy-start(s32[32]{0:T(128)} %param.12) | copy-start | bytes 388
Sparse Core Ops, SparseCore 0:
  9.6 83.4 all-gather.2
  95.0 57.2 all-gather.4
where the time goes:
time: 251 us; the launch traced here: 250 us
  waiting for transfers between devices  90.3 us (36%)
  matrix products  63.2 us (25%)
  blocking collectives  42.1 us (17%)
  local copies, waits for them, and re-layouts  20.7 us (8%)
  starting transfers between devices  18.8 us (7%)
  between operations  14.3 us (6%)
    all_to_all x1, waiting for transfers between devices, shards(): lax.all_to_all(outgoing_down, 'own', split_axis=0, concat_axis=0, tiled=T...  47.8 us
    psum x1, blocking collectives, shards(): inner_sum, q_sum = lax.psum((inner_part, q_part), 'fsdp')  42.1 us
    all_to_all x1, waiting for transfers between devices, shards(): lax.all_to_all(send_grad_a, 'own', split_axis=0, concat_axis=0, tiled=True)  41.1 us
    dot_general x6, matrix products, select_rows(): picked = jnp.dot(table, flat, preferred_element_type=jnp.bfloat16)  18.1 us
    dot_general x1, matrix products, shards(): lax.dot_general(full_grad, weight_rows, (((1,), (1,)), ((), ())), preferr...  15.1 us
    dot_general x1, local copies, waits for them, and re-layouts, shards(): jnp.einsum('btd,btr->bdr', x_blocks, q_blocks, preferred_element_type=jnp...  9.35 us
    dot_general x1, matrix products, shards(): jnp.einsum('jk,kdr->jdr', same_owner, part_a, precision=lax.Precision.HIG...  7.54 us
    dot_general x4, local copies, waits for them, and re-layouts, select_rows(): picked = jnp.dot(table, flat, preferred_element_type=jnp.bfloat16)  7.23 us
  transfers between devices with their start and end apart: 6, of which 2 were waited for; matrix products, arithmetic and copies ran while one was open for 28% of the time, Pallas kernels for 0%

commit v1 on v0

v1 whole, which is shorter than its diff:
```python
import jax
import jax.numpy as jnp
from jax import lax
from jax.experimental import pallas as pl
from jax.experimental.pallas import tpu as pltpu
from jax.sharding import PartitionSpec as P

KEY_VALUE_WIDTH = 1024
BLOCK = 128


def copy_body(index_ref, from_ref, to_ref):
    to_ref[...] = from_ref[...]


def pick_rows(index, stacked):
    shape = (1,) + stacked.shape[1:]
    return pl.pallas_call(
        copy_body,
        grid_spec=pltpu.PrefetchScalarGridSpec(
            num_scalar_prefetch=1,
            grid=(index.shape[0],),
            in_specs=[pl.BlockSpec(shape, lambda k, index_ref: (index_ref[k], 0, 0))],
            out_specs=pl.BlockSpec(shape, lambda k, index_ref: (k, 0, 0)),
        ),
        out_shape=jax.ShapeDtypeStruct(index.shape + stacked.shape[1:], stacked.dtype),
    )(index, stacked)


def inner_body(index_ref, x_ref, a_ref, out_ref):
    out_ref[...] = jnp.dot(x_ref[...], a_ref[0], preferred_element_type=jnp.float32).astype(
        out_ref.dtype
    )


def inner_product(index, tokens, maps):
    rows, width = tokens.shape
    rank = maps.shape[2]
    return pl.pallas_call(
        inner_body,
        grid_spec=pltpu.PrefetchScalarGridSpec(
            num_scalar_prefetch=1,
            grid=(index.shape[0],),
            in_specs=[
                pl.BlockSpec((BLOCK, width), lambda k, index_ref: (k, 0)),
                pl.BlockSpec((1, width, rank), lambda k, index_ref: (index_ref[k], 0, 0)),
            ],
            out_specs=pl.BlockSpec((BLOCK, rank), lambda k, index_ref: (k, 0)),
        ),
        out_shape=jax.ShapeDtypeStruct((rows, rank), jnp.bfloat16),
    )(index, tokens, maps)


def after(value, *others):
    return lax.optimization_barrier((value,) + others)[0]


def shards(
    activations, cotangent, frozen_weight, down_weight, up_weight, slot_of_adapter, tenant_of_block
):
    own_count = lax.axis_size("own")
    own_index = lax.axis_index("own")
    fsdp_count = lax.axis_size("fsdp")
    fsdp_index = lax.axis_index("fsdp")
    tok_rows, width_part = activations.shape
    col_count = cotangent.shape[1]
    resident_count = down_weight.shape[0]
    paired_rank = down_weight.shape[2]
    rank_half = paired_rank // 2
    block_count = tok_rows // BLOCK
    slot_table = slot_of_adapter[tenant_of_block].reshape(own_count, block_count)
    owner_table = slot_table // resident_count
    local_table = slot_table % resident_count
    wanted_mask = owner_table == own_index
    wanted_any = jnp.any(wanted_mask, axis=1)
    wanted_local = jnp.max(jnp.where(wanted_mask, local_table, 0), axis=1)
    held_ids = jnp.arange(resident_count, dtype=jnp.int32)
    serve_mask = (wanted_local[:, None] == held_ids[None, :]) & wanted_any[:, None]
    my_owner = lax.dynamic_index_in_dim(owner_table, own_index, 0, keepdims=False)
    owner_ids = jnp.arange(own_count, dtype=jnp.int32)
    owner_rows = jnp.repeat(my_owner, BLOCK)
    row_mask = owner_ids[:, None] == owner_rows[None, :]

    def exchange(value):
        return lax.all_to_all(value, "own", split_axis=0, concat_axis=0, tiled=True)

    fetched_b = exchange(pick_rows(wanted_local, up_weight))
    outgoing_down = after(pick_rows(wanted_local, down_weight), fetched_b)
    fetched_a = exchange(outgoing_down)

    g_blocks = cotangent.reshape(block_count, BLOCK, col_count)
    block_b = fetched_b[my_owner]
    q_single = jnp.einsum(
        "btc,brc->btr", g_blocks, block_b, preferred_element_type=jnp.float32
    ).reshape(tok_rows, rank_half)
    q_all = lax.all_gather(q_single.astype(jnp.bfloat16), "fsdp", axis=0)
    q_low = (
        q_all.reshape(2, fsdp_count // 2, tok_rows, rank_half)
        .astype(jnp.float32)
        .sum(axis=1)
        .astype(jnp.bfloat16)
    )
    q_low = jnp.concatenate([q_low[0], q_low[1]], axis=1)
    q_wide = jnp.where(row_mask[:, :, None], q_low[None], jnp.bfloat16(0))

    weight_rows = lax.all_gather(frozen_weight, "own", axis=1, tiled=True)
    full_grad = lax.all_gather(cotangent, "fsdp", axis=1, tiled=True)

    part_a = jnp.einsum(
        "otr,td->ord", q_wide, activations, preferred_element_type=jnp.float32
    ).astype(jnp.bfloat16)
    fetched_a, part_a, weight_rows = lax.optimization_barrier((fetched_a, part_a, weight_rows))
    back_a = exchange(part_a)

    inner_part = inner_product(my_owner, activations, fetched_a)
    inner_all = lax.all_gather(inner_part, "fsdp", axis=0)
    proj_index = fsdp_index * col_count // KEY_VALUE_WIDTH
    inner_mine = lax.dynamic_slice_in_dim(inner_all, proj_index * rank_half, rank_half, 2)
    inner_mine = inner_mine.astype(jnp.float32).sum(axis=0).astype(jnp.bfloat16)
    inner_wide = jnp.where(row_mask[:, :, None], inner_mine[None], jnp.bfloat16(0))
    part_b = jnp.einsum(
        "otr,tc->orc", inner_wide, cotangent, preferred_element_type=jnp.float32
    ).astype(jnp.bfloat16)

    block_a = fetched_a[my_owner]
    q_blocks = q_low.reshape(block_count, BLOCK, paired_rank)
    frozen_gradient = lax.dot_general(
        full_grad, weight_rows, (((1,), (1,)), ((), ())), preferred_element_type=jnp.float32
    )
    adapter_gradient = jnp.einsum(
        "mch,myh->mcy", q_blocks, block_a, preferred_element_type=jnp.float32
    ).reshape(tok_rows, width_part)
    activation_gradient = (frozen_gradient + adapter_gradient).astype(jnp.bfloat16)

    def accumulate(back):
        terms = jnp.where(serve_mask[:, :, None, None], back[:, None], jnp.bfloat16(0))
        return terms.astype(jnp.float32).sum(axis=0).astype(jnp.bfloat16)

    down_gradient = accumulate(after(back_a, activation_gradient)).transpose(0, 2, 1)
    back_b = exchange(after(part_b, back_a))
    up_gradient = accumulate(back_b)
    return (activation_gradient, down_gradient, up_gradient)


def solution(mesh):
    return jax.shard_map(
        shards,
        mesh=mesh,
        in_specs=(
            P("own", "fsdp"),
            P("own", "fsdp"),
            P("fsdp", "own"),
            P("own", "fsdp", None),
            P("own", None, "fsdp"),
            P(),
            P(),
        ),
        out_specs=(P("own", "fsdp"), P("own", "fsdp", None), P("own", None, "fsdp")),
        check_vma=False,
    )
```

time: 251 us -> 253 us (level)
  matrix products: 63.2 us -> 32.8 us
  blocking collectives: 42.1 us -> 16.4 us
  waiting for transfers between devices: 90.3 us -> 111 us
  Pallas kernels: 0 us -> 20.4 us
  other arithmetic: 1.13 us -> 11.4 us
  local copies, waits for them, and re-layouts: 20.7 us -> 25.7 us
    all_gather x1, waiting for transfers between devices: 0.01 us -> 49.6 us  [shards(): full_grad = lax.all_gather(cotangent, 'fsdp', axis=1, tiled=True)]
    psum x1 -> x0, blocking collectives: 42.1 us -> none  [shards(): inner_sum, q_sum = lax.psum((inner_part, q_part), 'fsdp')]
    all_to_all x4, waiting for transfers between devices: 88.9 us -> 54.1 us  [exchange(): return lax.all_to_all(value, 'own', split_axis=0, concat_axis=0, tiled=True)]
    dot_general x13 -> x2, matrix products: 40.9 us -> 9.78 us  [the longest x1 8.28 us: shards(): jnp.einsum('otr,td->ord', q_wide, activations, preferred_element_type=jnp...]
    pallas_call x0 -> x3, Pallas kernels: none -> 20.4 us  [the longest x2 12.1 us: pick_rows(): pl.pallas_call(copy_body, grid_spec=pltpu.PrefetchScalarGridSpec(num_scal...]
    dot_general x5 -> x0, local copies, waits for them, and re-layouts: 16.6 us -> none  [the longest x1 9.35 us: shards(): jnp.einsum('btd,btr->bdr', x_blocks, q_blocks, preferred_element_type=jnp...]
    all_gather x0 -> x1, blocking collectives: none -> 16.4 us  [shards(): q_all = lax.all_gather(q_single.astype(jnp.bfloat16), 'fsdp', axis=0)]
    reduce_sum x0 -> x4, other arithmetic: none -> 9.85 us  [the longest x2 8.14 us: accumulate(): return terms.astype(jnp.float32).sum(axis=0).astype(jnp.bfloat16)]
  transfers between devices with their start and end apart: 6 -> 7, of which waited for: 2 -> 5; matrix products, arithmetic and copies ran while one was open for 28% -> 27% of each run, Pallas kernels for 0% -> 8%
where the time goes in v1:
time: 253 us; the launch traced here: 251 us
  waiting for transfers between devices  111 us (44%)
  matrix products  32.8 us (13%)
  local copies, waits for them, and re-layouts  25.7 us (10%)
  Pallas kernels  20.4 us (8%)
  starting transfers between devices  19.1 us (8%)
  blocking collectives  16.4 us (6%)
  between operations  13.9 us (5%)
  other arithmetic  11.4 us (5%)
    all_to_all x4, waiting for transfers between devices, exchange(): return lax.all_to_all(value, 'own', split_axis=0, concat_axis=0, tiled=True)  54.1 us
    all_gather x1, waiting for transfers between devices, shards(): full_grad = lax.all_gather(cotangent, 'fsdp', axis=1, tiled=True)  49.6 us
    all_to_all x4, starting transfers between devices, exchange(): return lax.all_to_all(value, 'own', split_axis=0, concat_axis=0, tiled=True)  18.8 us
    all_gather x1, blocking collectives, shards(): q_all = lax.all_gather(q_single.astype(jnp.bfloat16), 'fsdp', axis=0)  16.4 us
    dot_general x1, matrix products, shards(): lax.dot_general(full_grad, weight_rows, (((1,), (1,)), ((), ())), preferr...  15.8 us
    pallas_call x2, Pallas kernels, pick_rows(): pl.pallas_call(copy_body, grid_spec=pltpu.PrefetchScalarGridSpec(num_scal...  12.1 us
    reshape x1, local copies, waits for them, and re-layouts, shards(): adapter_gradient = jnp.einsum('mch,myh->mcy', q_blocks, block_a, preferre...  9.27 us
    unnamed x12, local copies, waits for them, and re-layouts  8.95 us
  transfers between devices with their start and end apart: 7, of which 5 were waited for; matrix products, arithmetic and copies ran while one was open for 27% of the time, Pallas kernels for 8%

profile of v1, /device:TPU:0, one launch (start us, length us, event | category | flops | bytes accessed | tf_op | source)
XLA Modules:
  0.0 251.3 jit_solution(9806081319206455175)
XLA Ops:
  7.2 0.0 copy-start
  7.2 0.0 all-gather.5.cloned.1.call-start
  7.2 0.7 all-gather.5.cloned.1.call-update
  7.9 0.0 all-gather.7.cloned.1.call-start
  8.0 0.7 all-gather.7.cloned.1.call-update
  8.7 0.7 compare_select_fusion.1
  9.3 0.0 copy-done
  9.3 0.8 gather_fusion
  10.1 0.1 reshape.125
  10.2 0.1 fusion.30
  10.3 0.6 fusion.21.index_ref
  11.0 5.2 %shard_map.95 = bf16[8,64,512]{2,1,0:T(8,128)(2,1)} custom-call(s32[8]{0:T(128)} %fusion.21.index_ref, bf16[4,64,512]{2,1,0:T(8,128)(2,1)} %from_ref.3), custom_call_target="tpu_custom_call" | custom-call | tf_op jit(solution)/shard_map/pallas_call | solution.py:18
  16.1 5.2 %all-to-all-start = ((bf16[8,64,512]{2,1,0:T(8,128)(2,1)}), bf16[8,64,512]{2,1,0:T(8,128)(2,1)S(1)}, u32[]{:S(2)}, u32[]{:S(2)}) async-start(bf16[8,64,512]{2,1,0:T(8,128)(2,1)} %shard_map.95), calls=%async_computation | async-start | bytes 1048576 | tf_op jit(solution)/shard_map/all_to_all | solution.py:85
  21.3 6.9 %shard_map.94 = bf16[8,2048,128]{2,1,0:T(8,128)(2,1)} custom-call(s32[8]{0:T(128)} %fusion.21.index_ref, bf16[4,2048,128]{2,1,0:T(8,128)(2,1)} %from_ref.2), custom_call_target="tpu_custom_call" | custom-call | tf_op jit(solution)/shard_map/pallas_call | solution.py:18
  28.2 0.0 copy-start.2
  28.2 8.7 %all-to-all-done = bf16[8,64,512]{2,1,0:T(8,128)(2,1)S(1)} async-done(((bf16[8,64,512]{2,1,0:T(8,128)(2,1)}), bf16[8,64,512]{2,1,0:T(8,128)(2,1)S(1)}, u32[]{:S(2)}, u32[]{:S(2)}) %all-to-all-start) | async-done | bytes 524320 | tf_op jit(solution)/shard_map/all_to_all | solution.py:85
  36.9 4.6 %all-to-all-start.1 = ((bf16[8,2048,128]{2,1,0:T(8,128)(2,1)}), bf16[8,2048,128]{2,1,0:T(8,128)(2,1)}, u32[]{:S(2)}, u32[]{:S(2)}) async-start(bf16[8,2048,128]{2,1,0:T(8,128)(2,1)} %shard_map.94), calls=%async_computation.1 | async-start | bytes 8388608 | tf_op jit(solution)/shard_map/all_to_all | solution.py:85
  41.5 0.0 copy-start.4
  41.6 0.1 broadcast_bitcast_fusion
  41.6 0.6 gather_fusion.1
  42.2 0.0 copy-done.2
  42.2 0.5 fusion.8
  42.7 0.1 copy.23
  42.8 0.1 convert_element_type.35
  42.9 16.4 %all_gather.16 = bf16[4,1024,64]{1,2,0:T(8,128)(2,1)S(1)} all-gather(bf16[1,1024,64]{1,2,0:T(8,128)(2,1)S(1)} %convert_element_type.35), channel_id=1, replica_groups=mesh['fsdp'=4,'own'=8] {'fsdp'}, dimensions={0}, use_global_device_ids=true | all-gather | bytes 655360 | tf_op jit(solution)/shard_map/all_gather | solution.py:96
  59.3 0.1 bitcast_reduce_fusion
  59.4 0.1 fusion.31
  59.5 8.3 %fusion.3 = bf16[8,128,2048]{2,1,0:T(8,128)(2,1)} fusion(bf16[1024,2048]{1,0:T(8,128)(2,1)} %x_ref.1, pred[8,1024]{1,0:T(8,128)(4,1)S(1)} %iota_compare_fusion, bf16[1024,128]{0,1:T(8,128)(2,1)S(1)} %pad_maximum_fusion), kind=kOutput, calls=%fused_computation.8 | convolution fusion | flops 4298113024 | bytes 8658944 | tf_op jit(solution)/shard_map/otr,td->ord/dot_general | solution.py:109
  67.8 0.0 copy-done.4
  67.8 0.0 copy-start.3
  67.8 45.3 %all-to-all-done.1.a_ref = bf16[8,2048,128]{2,1,0:T(8,128)(2,1)} async-done(((bf16[8,2048,128]{2,1,0:T(8,128)(2,1)}), bf16[8,2048,128]{2,1,0:T(8,128)(2,1)}, u32[]{:S(2)}, u32[]{:S(2)}) %all-to-all-start.1) | async-done | bytes 4194336 | tf_op jit(solution)/shard_map/all_to_all | solution.py:85
  113.0 0.0 all-gather.5.cloned.1.call-done
  113.0 5.4 %all-to-all-start.2 = ((bf16[8,128,2048]{2,1,0:T(8,128)(2,1)}), bf16[8,128,2048]{2,1,0:T(8,128)(2,1)}, u32[]{:S(2)}, u32[]{:S(2)}) async-start(bf16[8,128,2048]{2,1,0:T(8,128)(2,1)} %fusion.3), calls=%async_computation.2 | async-start | bytes 8388608 | tf_op jit(solution)/shard_map/all_to_all | solution.py:85
  118.4 0.2 all-gather.9.cloned.1.call-start
  118.7 0.0 copy-done.3
  118.7 0.1 fusion.23
  118.8 0.2 copy.24
  118.9 0.2 copy.25
  119.1 5.3 %gather_fusion.2 = bf16[8,2048,128]{2,1,0:T(8,128)(2,1)} fusion(bf16[8,2048,128]{2,1,0:T(8,128)(2,1)} %all-to-all-done.1.a_ref, s32[1024]{0:T(1024)S(1)} %pad_clamp_fusion), kind=kCustom, calls=%fused_computation.2 | custom fusion | bytes 8388640 | tf_op jit(solution)/shard_map/gather | solution.py:125
  124.4 8.3 %shard_map.96 = bf16[1024,128]{1,0:T(8,128)(2,1)} custom-call(s32[8]{0:T(128)} %copy-done.4, bf16[1024,2048]{1,0:T(8,128)(2,1)} %x_ref.1, bf16[8,2048,128]{2,1,0:T(8,128)(2,1)} %all-to-all-done.1.a_ref), custom_call_target="tpu_custom_call" | custom-call | tf_op jit(solution)/shard_map/pallas_call | solution.py:39
  132.7 6.7 %fusion.16 = f32[8,128,2048]{2,1,0:T(8,128)} fusion(bf16[8,2048,128]{2,1,0:T(8,128)(2,1)} %gather_fusion.2, bf16[8,128,64]{2,1,0:T(8,128)(2,1)S(1)} %bitcast.45, bf16[8,128,64]{2,1,0:T(8,128)(2,1)S(1)} %bitcast.44), kind=kOutput, calls=%fused_computation.25 | convolution fusion | flops 537395200 | bytes 12845056 | tf_op jit(solution)/shard_map/mch,myh->mcy/dot_general | solution.py:130
  139.5 9.3 %copy.30 = f32[1024,2048]{0,1:T(8,128)} copy(f32[1024,2048]{1,0:T(8,128)} %bitcast.41) | data formatting | bytes 16777216 | tf_op jit(solution)/shard_map/reshape | solution.py:132
  148.8 0.0 all-gather.9.cloned.1.call-update
  148.8 49.6 %all-gather.7.cloned.1.call-done = bf16[1024,2048]{1,0:T(8,128)(2,1)} async-done(((bf16[1024,512]{1,0:T(8,128)(2,1)}), bf16[1024,2048]{1,0:T(8,128)(2,1)}) %all-gather.7.cloned.1.call-update) | async-done | bytes 4194320 | tf_op jit(solution)/shard_map/all_gather | solution.py:107
  198.4 15.8 %fusion = bf16[1024,2048]{0,1:T(8,128)(2,1)} fusion(f32[1024,2048]{0,1:T(8,128)} %copy.30, bf16[2048,2048]{1,0:T(8,128)(2,1)} %all-gather.5.cloned.1.call-done, bf16[1024,2048]{1,0:T(8,128)(2,1)} %all-gather.7.cloned.1.call-done), kind=kOutput, calls=%fused_computation.5 | convolution fusion | flops 8594128896 | bytes 25165824 | tf_op jit(solution)/shard_map/dot_general | solution.py:127
  214.1 6.4 %copy.28 = bf16[1024,2048]{1,0:T(8,128)(2,1)} copy(bf16[1024,2048]{0,1:T(8,128)(2,1)} %fusion) | data formatting | bytes 8388608
  220.6 6.4 %all-gather.9.cloned.1.call-done = bf16[4096,128]{1,0:T(8,128)(2,1)} async-done(((bf16[1024,128]{1,0:T(8,128)(2,1)}), bf16[4096,128]{1,0:T(8,128)(2,1)}) %all-gather.9.cloned.1.call-update) | async-done | bytes 1048592 | tf_op jit(solution)/shard_map/all_gather | solution.py:116
  227.0 1.6 dynamic-slice_reduce_fusion
  228.7 0.1 copy.27
  228.8 1.5 convolution_convert_fusion
  230.3 0.0 all-to-all-done.2
  230.3 3.7 %all-to-all-start.3 = ((bf16[8,64,512]{2,1,0:T(8,128)(2,1)}), bf16[8,64,512]{2,1,0:T(8,128)(2,1)S(1)}, u32[]{:S(2)}, u32[]{:S(2)}) async-start(bf16[8,64,512]{2,1,0:T(8,128)(2,1)} %convolution_convert_fusion), calls=%async_computation.3 | async-start | bytes 1048576 | tf_op jit(solution)/shard_map/all_to_all | solution.py:85
  234.0 0.0 copy-start.1
  234.0 7.1 %select_reduce_fusion = bf16[4,128,2048]{2,1,0:T(8,128)(2,1)S(1)} fusion(pred[8,4]{1,0:T(8,128)(4,1)S(1)} %fusion.23, bf16[8,128,2048]{2,1,0:T(8,128)(2,1)} %all-to-all-done.2), kind=kLoop, calls=%fused_computation.3 | loop fusion | flops 15728640 | bytes 6291488 | tf_op jit(solution)/shard_map/reduce_sum | solution.py:137
  241.1 2.5 copy.29
  243.6 0.1 all-to-all-done.3
  243.7 1.1 select_reduce_fusion.1
  244.8 0.0 copy-done.1
  (6 shorter events, 0.1 us)
Async XLA Ops:
  7.2 2.2 copy-start
  7.2 105.9 %all-gather.5.cloned.1.call-start = ((), (), s32[]{:S(2)}) async-start(), calls=%async_computation.4 | async-start | bytes 9437184 | tf_op jit(solution)/shard_map/all_gather | solution.py:106
  7.9 190.5 %all-gather.7.cloned.1.call-start = ((), (), s32[]{:S(2)}) async-start(), calls=%async_computation.5 | async-start | bytes 5242880 | tf_op jit(solution)/shard_map/all_gather | solution.py:107
  16.1 20.8 %all-to-all-start = ((bf16[8,64,512]{2,1,0:T(8,128)(2,1)}), bf16[8,64,512]{2,1,0:T(8,128)(2,1)S(1)}, u32[]{:S(2)}, u32[]{:S(2)}) async-start(bf16[8,64,512]{2,1,0:T(8,128)(2,1)} %shard_map.95), calls=%async_computation | async-start | bytes 1048576 | tf_op jit(solution)/shard_map/all_to_all | solution.py:85
  28.2 14.0 %copy-start.2 = (bf16[1024,512]{1,0:T(8,128)(2,1)S(1)}, bf16[1024,512]{1,0:T(8,128)(2,1)}, u32[]{:S(2)}) copy-start(bf16[1024,512]{1,0:T(8,128)(2,1)} %param.8) | copy-start | bytes 3145732
  36.9 76.1 %all-to-all-start.1 = ((bf16[8,2048,128]{2,1,0:T(8,128)(2,1)}), bf16[8,2048,128]{2,1,0:T(8,128)(2,1)}, u32[]{:S(2)}, u32[]{:S(2)}) async-start(bf16[8,2048,128]{2,1,0:T(8,128)(2,1)} %shard_map.94), calls=%async_computation.1 | async-start | bytes 8388608 | tf_op jit(solution)/shard_map/all_to_all | solution.py:85
  41.5 26.2 %copy-start.4 = (s32[8]{0:T(128)}, s32[8]{0:T(128)S(1)}, u32[]{:S(2)}) copy-start(s32[8]{0:T(128)S(1)} %fusion.26.index_ref) | copy-start | bytes 100
  67.8 50.9 %copy-start.3 = (s32[8]{0:T(128)S(1)}, s32[8]{0:T(128)}, u32[]{:S(2)}) copy-start(s32[8]{0:T(128)} %fusion.21.index_ref) | copy-start | bytes 100
  113.0 117.3 %all-to-all-start.2 = ((bf16[8,128,2048]{2,1,0:T(8,128)(2,1)}), bf16[8,128,2048]{2,1,0:T(8,128)(2,1)}, u32[]{:S(2)}, u32[]{:S(2)}) async-start(bf16[8,128,2048]{2,1,0:T(8,128)(2,1)} %fusion.3), calls=%async_computation.2 | async-start | bytes 8388608 | tf_op jit(solution)/shard_map/all_to_all | solution.py:85
  118.4 108.6 %all-gather.9.cloned.1.call-start = ((), (), s32[]{:S(2)}) async-start(), calls=%async_computation.6 | async-start | bytes 1310720 | tf_op jit(solution)/shard_map/all_gather | solution.py:116
  230.3 13.4 %all-to-all-start.3 = ((bf16[8,64,512]{2,1,0:T(8,128)(2,1)}), bf16[8,64,512]{2,1,0:T(8,128)(2,1)S(1)}, u32[]{:S(2)}, u32[]{:S(2)}) async-start(bf16[8,64,512]{2,1,0:T(8,128)(2,1)} %convolution_convert_fusion), calls=%async_computation.3 | async-start | bytes 1048576 | tf_op jit(solution)/shard_map/all_to_all | solution.py:85
  234.0 10.8 %copy-start.1 = (s32[32]{0:T(128)S(1)}, s32[32]{0:T(128)}, u32[]{:S(2)}) copy-start(s32[32]{0:T(128)} %param.12) | copy-start | bytes 388
Sparse Core Ops, SparseCore 0:
  9.9 94.5 all-gather.4
  106.0 92.2 all-gather.6
  200.5 26.4 all-gather.8

commit v2 on v1

--- a/solution.py
+++ b/solution.py
@@ -1,3 +1,5 @@
+import functools
+
 import jax
 import jax.numpy as jnp
 from jax import lax
@@ -7,6 +9,7 @@
 
 KEY_VALUE_WIDTH = 1024
 BLOCK = 128
+MESH = pl.DeviceIdType.MESH
 
 
 def copy_body(index_ref, from_ref, to_ref):
@@ -49,6 +52,221 @@
         ),
         out_shape=jax.ShapeDtypeStruct((rows, rank), jnp.bfloat16),
     )(index, tokens, maps)
+
+
+def gather_body(chips, ring, w_ref, g_ref, w_out, g_out, w_send, w_recv, f_send, f_recv, g_send, g_recv, here):
+    own = lax.axis_index("own")
+    fsdp = lax.axis_index("fsdp")
+    chip, core = own // 2, lax.rem(own, 2)
+    sibling = chip * 2 + 1 - core
+    columns = g_ref.shape[1]
+
+    def chip_of(k):
+        return lax.rem(chip + k, chips)
+
+    def g_slice(f):
+        return g_out.at[:, pl.ds(pl.multiple_of(f * columns, columns), columns)]
+
+    keep_w = pltpu.make_async_copy(w_ref, w_out.at[own], here.at[0])
+    keep_g = pltpu.make_async_copy(g_ref, g_slice(fsdp), here.at[1])
+    keep_w.start()
+    keep_g.start()
+
+    barrier = pltpu.get_barrier_semaphore()
+    for k in range(1, chips):
+        pl.semaphore_signal(
+            barrier, inc=1, device_id={"own": chip_of(k) * 2 + core}, device_id_type=MESH
+        )
+    pl.semaphore_signal(barrier, inc=1, device_id={"own": sibling}, device_id_type=MESH)
+
+    @pl.when(fsdp > 0)
+    def _():
+        pl.semaphore_signal(barrier, inc=1, device_id={"fsdp": fsdp - 1}, device_id_type=MESH)
+
+    @pl.when(fsdp < ring - 1)
+    def _():
+        pl.semaphore_signal(barrier, inc=1, device_id={"fsdp": fsdp + 1}, device_id_type=MESH)
+
+    inside = (fsdp > 0).astype(jnp.int32) + (fsdp < ring - 1).astype(jnp.int32)
+    pl.semaphore_wait(barrier, chips + inside)
+
+    def g_copy(way, k):
+        sign = 1 if way == 0 else -1
+        origin = fsdp - sign * k
+        return pltpu.make_async_remote_copy(
+            src_ref=g_ref if k == 0 else g_slice(origin),
+            dst_ref=g_slice(origin),
+            send_sem=g_send.at[way, k],
+            recv_sem=g_recv.at[way, k],
+            device_id={"fsdp": fsdp + sign},
+            device_id_type=MESH,
+        )
+
+    def g_arrival(way, k):
+        sign = 1 if way == 0 else -1
+        origin = fsdp - sign * (k + 1)
+        return pltpu.make_async_remote_copy(
+            src_ref=g_slice(origin),
+            dst_ref=g_slice(origin),
+            send_sem=g_send.at[way, k],
+            recv_sem=g_recv.at[way, k],
+            device_id={"fsdp": fsdp - sign},
+            device_id_type=MESH,
+        )
+
+    def g_sends(way, k):
+        if way == 0:
+            return (fsdp >= k) & (fsdp < ring - 1)
+        return (fsdp <= ring - 1 - k) & (fsdp > 0)
+
+    def g_gets(way, k):
+        return fsdp >= k + 1 if way == 0 else fsdp <= ring - 2 - k
+
+    def w_copy(k):
+        return pltpu.make_async_remote_copy(
+            src_ref=w_ref,
+            dst_ref=w_out.at[own],
+            send_sem=w_send.at[k - 1],
+            recv_sem=w_recv.at[k - 1],
+            device_id={"own": chip_of(k) * 2 + core},
+            device_id_type=MESH,
+        )
+
+    def w_origin(k, side):
+        return lax.rem(chip + chips - k, chips) * 2 + side
+
+    def w_forward(k):
+        piece = w_origin(k, core)
+        return pltpu.make_async_remote_copy(
+            src_ref=w_ref if k == 0 else w_out.at[piece],
+            dst_ref=w_out.at[piece],
+            send_sem=f_send.at[k],
+            recv_sem=f_recv.at[k],
+            device_id={"own": sibling},
+            device_id_type=MESH,
+        )
+
+    for way in range(2):
+        @pl.when(g_sends(way, 0))
+        def _():
+            g_copy(way, 0).start()
+
+    for k in range(1, chips):
+        w_copy(k).start()
+    w_forward(0).start()
+
+    for k in range(max(ring - 1, chips - 1)):
+        if k < ring - 1:
+            for way in range(2):
+                @pl.when(g_gets(way, k))
+                def _():
+                    g_arrival(way, k).wait_recv()
+
+                if k + 1 < ring - 1:
+                    @pl.when(g_sends(way, k + 1))
+                    def _():
+                        g_copy(way, k + 1).start()
+        if k < chips - 1:
+            piece = w_origin(k + 1, core)
+            pltpu.make_async_remote_copy(
+                src_ref=w_ref,
+                dst_ref=w_out.at[piece],
+                send_sem=w_send.at[k],
+                recv_sem=w_recv.at[k],
+                device_id={"own": sibling},
+                device_id_type=MESH,
+            ).wait_recv()
+            w_forward(k + 1).start()
+
+    for k in range(chips):
+        piece = w_origin(k, 1 - core)
+        pltpu.make_async_remote_copy(
+            src_ref=w_ref,
+            dst_ref=w_out.at[piece],
+            send_sem=f_send.at[k],
+            recv_sem=f_recv.at[k],
+            device_id={"own": sibling},
+            device_id_type=MESH,
+        ).wait_recv()
+        w_forward(k).wait_send()
+    for k in range(1, chips):
+        w_copy(k).wait_send()
+    for k in range(ring - 1):
+        for way in range(2):
+            @pl.when(g_sends(way, k))
+            def _():
+                g_copy(way, k).wait_send()
+    keep_w.wait()
+    keep_g.wait()
+
+
+def gather(weight, cotangent):
+    own_count, ring = lax.axis_size("own"), lax.axis_size("fsdp")
+    chips = own_count // 2
+    hbm = pl.BlockSpec(memory_space=pl.ANY)
+    dma = pltpu.SemaphoreType.DMA
+    return pl.pallas_call(
+        functools.partial(gather_body, chips, ring),
+        out_shape=(
+            jax.ShapeDtypeStruct((own_count,) + weight.shape, weight.dtype),
+            jax.ShapeDtypeStruct((cotangent.shape[0], cotangent.shape[1] * ring), cotangent.dtype),
+        ),
+        in_specs=[hbm, hbm],
+        out_specs=(hbm, hbm),
+        scratch_shapes=[
+            dma((chips - 1,)),
+            dma((chips - 1,)),
+            dma((chips,)),
+            dma((chips,)),
+            dma((2, ring - 1)),
+            dma((2, ring - 1)),
+            dma((2,)),
+        ],
+        compiler_params=pltpu.CompilerParams(collective_id=0, has_side_effects=True),
+    )(weight, cotangent)
+
+
+def grad_body(index_ref, g_ref, w_ref, a_ref, q_ref, out_ref, total):
+    weight = jnp.concatenate([w_ref[o] for o in range(w_ref.shape[0])], axis=1)
+    contract_last = (((1,), (1,)), ((), ()))
+    total[...] = lax.dot_general(
+        g_ref[...], weight, contract_last, preferred_element_type=jnp.float32
+    )
+    for j in range(out_ref.shape[0] // BLOCK):
+        rows = pl.ds(j * BLOCK, BLOCK)
+        extra = lax.dot_general(
+            q_ref[rows, :], a_ref[index_ref[j]], contract_last, preferred_element_type=jnp.float32
+        )
+        out_ref[rows, :] = (total[rows, :] + extra).astype(out_ref.dtype)
+
+
+def activation_grad(index, cotangent, weight, maps, q_low):
+    rows, columns = cotangent.shape
+    own_count, width, piece = weight.shape
+    rank = maps.shape[2]
+    tile = 256
+    return pl.pallas_call(
+        grad_body,
+        grid_spec=pltpu.PrefetchScalarGridSpec(
+            num_scalar_prefetch=1,
+            grid=(width // tile,),
+            in_specs=[
+                pl.BlockSpec((rows, columns), lambda k, index_ref: (0, 0)),
+                pl.BlockSpec((own_count, tile, piece), lambda k, index_ref: (0, k, 0)),
+                pl.BlockSpec((own_count, tile, rank), lambda k, index_ref: (0, k, 0)),
+                pl.BlockSpec((rows, rank), lambda k, index_ref: (0, 0)),
+            ],
+            out_specs=pl.BlockSpec((rows, tile), lambda k, index_ref: (0, k)),
+            scratch_shapes=[pltpu.VMEM((rows, tile), jnp.float32)],
+        ),
+        out_shape=jax.ShapeDtypeStruct((rows, width), jnp.bfloat16),
+        compiler_params=pltpu.CompilerParams(vmem_limit_bytes=40 * 1024 * 1024),
+        cost_estimate=pl.CostEstimate(
+            flops=2 * rows * width * (columns + rank),
+            bytes_accessed=2 * (rows * columns + width * columns + rows * width),
+            transcendentals=0,
+        ),
+    )(index, cotangent, weight, maps, q_low)
 
 
 def after(value, *others):
@@ -103,12 +321,13 @@
     q_low = jnp.concatenate([q_low[0], q_low[1]], axis=1)
     q_wide = jnp.where(row_mask[:, :, None], q_low[None], jnp.bfloat16(0))
 
-    weight_rows = lax.all_gather(frozen_weight, "own", axis=1, tiled=True)
-    full_grad = lax.all_gather(cotangent, "fsdp", axis=1, tiled=True)
-
     part_a = jnp.einsum(
         "otr,td->ord", q_wide, activations, preferred_element_type=jnp.float32
     ).astype(jnp.bfloat16)
+    late_weight, late_cotangent, part_a, outgoing_down = lax.optimization_barrier(
+        (frozen_weight, cotangent, part_a, outgoing_down)
+    )
+    weight_rows, full_grad = gather(late_weight, late_cotangent)
     fetched_a, part_a, weight_rows = lax.optimization_barrier((fetched_a, part_a, weight_rows))
     back_a = exchange(part_a)
 
@@ -122,15 +341,7 @@
         "otr,tc->orc", inner_wide, cotangent, preferred_element_type=jnp.float32
     ).astype(jnp.bfloat16)
 
-    block_a = fetched_a[my_owner]
-    q_blocks = q_low.reshape(block_count, BLOCK, paired_rank)
-    frozen_gradient = lax.dot_general(
-        full_grad, weight_rows, (((1,), (1,)), ((), ())), preferred_element_type=jnp.float32
-    )
-    adapter_gradient = jnp.einsum(
-        "mch,myh->mcy", q_blocks, block_a, preferred_element_type=jnp.float32
-    ).reshape(tok_rows, width_part)
-    activation_gradient = (frozen_gradient + adapter_gradient).astype(jnp.bfloat16)
+    activation_gradient = activation_grad(my_owner, full_grad, weight_rows, fetched_a, q_low)
 
     def accumulate(back):
         terms = jnp.where(serve_mask[:, :, None, None], back[:, None], jnp.bfloat16(0))

time: 253 us -> 215 us (0.85)
  Pallas kernels: 20.4 us -> 108 us
  waiting for transfers between devices: 111 us -> 24.3 us
  matrix products: 32.8 us -> 10.2 us
  local copies, waits for them, and re-layouts: 25.7 us -> 7.04 us
    pallas_call x0 -> x2, Pallas kernels: none -> 88.4 us  [the longest x1 73.7 us: gather(): pl.pallas_call(functools.partial(gather_body, chips, ring), out_shape=(ja...]
    all_gather x2 -> x0, waiting for transfers between devices: 49.6 us -> none  [the longest x1 49.6 us: shards(): full_grad = lax.all_gather(cotangent, 'fsdp', axis=1, tiled=True)]
    all_to_all x4, waiting for transfers between devices: 54.1 us -> 14 us  [exchange(): return lax.all_to_all(value, 'own', split_axis=0, concat_axis=0, tiled=True)]
    dot_general x2 -> x0, matrix products: 22.5 us -> none  [the longest x1 15.8 us: shards(): lax.dot_general(full_grad, weight_rows, (((1,), (1,)), ((), ())), preferr...]
    reshape x1 -> x0, local copies, waits for them, and re-layouts: 9.27 us -> none  [shards(): adapter_gradient = jnp.einsum('mch,myh->mcy', q_blocks, block_a, preferre...]
    gather x1 -> x0, local copies, waits for them, and re-layouts: 5.29 us -> none  [shards(): block_a = fetched_a[my_owner]]
    unnamed x12 -> x17, local copies, waits for them, and re-layouts: 8.95 us -> 5.07 us
    all_gather x1, waiting for transfers between devices: 6.45 us -> 10.2 us  [shards(): inner_all = lax.all_gather(inner_part, 'fsdp', axis=0)]
  transfers between devices with their start and end apart: 7 -> 5, of which waited for: 5 -> 3; matrix products, arithmetic and copies ran while one was open for 27% -> 11% of each run, Pallas kernels for 8% -> 48%
where the time goes in v2:
time: 215 us; the launch traced here: 213 us
  Pallas kernels  108 us (50%)
  waiting for transfers between devices  24.3 us (11%)
  starting transfers between devices  21.4 us (10%)
  blocking collectives  16.4 us (8%)
  between operations  14.3 us (7%)
  other arithmetic  11.6 us (5%)
  matrix products  10.2 us (5%)
  local copies, waits for them, and re-layouts  7.04 us (3%)
    pallas_call x1, Pallas kernels, gather(): pl.pallas_call(functools.partial(gather_body, chips, ring), out_shape=(ja...  73.7 us
    all_to_all x4, starting transfers between devices, exchange(): return lax.all_to_all(value, 'own', split_axis=0, concat_axis=0, tiled=True)  21.4 us
    all_gather x1, blocking collectives, shards(): q_all = lax.all_gather(q_single.astype(jnp.bfloat16), 'fsdp', axis=0)  16.4 us
    pallas_call x1, Pallas kernels, activation_grad(): pl.pallas_call(grad_body, grid_spec=pltpu.PrefetchScalarGridSpec(num_scal...  14.7 us
    all_to_all x4, waiting for transfers between devices, exchange(): return lax.all_to_all(value, 'own', split_axis=0, concat_axis=0, tiled=True)  14 us
    pallas_call x2, Pallas kernels, pick_rows(): pl.pallas_call(copy_body, grid_spec=pltpu.PrefetchScalarGridSpec(num_scal...  11.9 us
    all_gather x1, waiting for transfers between devices, shards(): inner_all = lax.all_gather(inner_part, 'fsdp', axis=0)  10.2 us
    dot_general x1, matrix products, shards(): jnp.einsum('otr,td->ord', q_wide, activations, preferred_element_type=jnp...  8.24 us
  transfers between devices with their start and end apart: 5, of which 3 were waited for; matrix products, arithmetic and copies ran while one was open for 11% of the time, Pallas kernels for 48%

profile of v2, /device:TPU:0, one launch (start us, length us, event | category | flops | bytes accessed | tf_op | source)
XLA Modules:
  0.0 213.5 jit_solution(8457936258054529474)
XLA Ops:
  7.2 0.0 copy-start
  7.2 0.7 compare_select_fusion.1
  7.9 0.0 copy-done
  7.9 0.8 gather_fusion
  8.6 0.1 reshape.117
  8.7 0.1 fusion.24
  8.8 0.7 fusion.16.index_ref
  9.5 5.1 %shard_map.94 = bf16[8,64,512]{2,1,0:T(8,128)(2,1)} custom-call(s32[8]{0:T(128)} %fusion.16.index_ref, bf16[4,64,512]{2,1,0:T(8,128)(2,1)} %from_ref.2), custom_call_target="tpu_custom_call" | custom-call | tf_op jit(solution)/shard_map/pallas_call | solution.py:21
  14.6 5.4 %all-to-all-start = ((bf16[8,64,512]{2,1,0:T(8,128)(2,1)}), bf16[8,64,512]{2,1,0:T(8,128)(2,1)S(1)}, u32[]{:S(2)}, u32[]{:S(2)}) async-start(bf16[8,64,512]{2,1,0:T(8,128)(2,1)} %shard_map.94), calls=%async_computation | async-start | bytes 1048576 | tf_op jit(solution)/shard_map/all_to_all | solution.py:303
  20.1 6.8 %shard_map.95 = bf16[8,2048,128]{2,1,0:T(8,128)(2,1)} custom-call(s32[8]{0:T(128)} %fusion.16.index_ref, bf16[4,2048,128]{2,1,0:T(8,128)(2,1)} %from_ref.3), custom_call_target="tpu_custom_call" | custom-call | tf_op jit(solution)/shard_map/pallas_call | solution.py:21
  26.8 0.0 copy-start.4
  26.8 3.0 %all-to-all-done = bf16[8,64,512]{2,1,0:T(8,128)(2,1)S(1)} async-done(((bf16[8,64,512]{2,1,0:T(8,128)(2,1)}), bf16[8,64,512]{2,1,0:T(8,128)(2,1)S(1)}, u32[]{:S(2)}, u32[]{:S(2)}) %all-to-all-start) | async-done | bytes 524320 | tf_op jit(solution)/shard_map/all_to_all | solution.py:303
  29.8 4.5 %all-to-all-start.1 = ((bf16[8,2048,128]{2,1,0:T(8,128)(2,1)}), bf16[8,2048,128]{2,1,0:T(8,128)(2,1)}, u32[]{:S(2)}, u32[]{:S(2)}) async-start(bf16[8,2048,128]{2,1,0:T(8,128)(2,1)} %shard_map.95), calls=%async_computation.1 | async-start | bytes 8388608 | tf_op jit(solution)/shard_map/all_to_all | solution.py:303
  34.4 0.0 copy-start.1
  34.4 0.1 broadcast_bitcast_fusion
  34.5 0.6 gather_fusion.1
  35.1 0.0 copy-done.4
  35.1 0.5 fusion.7
  35.6 0.1 copy.18
  35.7 0.1 convert_element_type.32
  35.8 16.4 %all_gather.10 = bf16[4,1024,64]{1,2,0:T(8,128)(2,1)S(1)} all-gather(bf16[1,1024,64]{1,2,0:T(8,128)(2,1)S(1)} %convert_element_type.32), channel_id=1, replica_groups=mesh['fsdp'=4,'own'=8] {'fsdp'}, dimensions={0}, use_global_device_ids=true | all-gather | bytes 655360 | tf_op jit(solution)/shard_map/all_gather | solution.py:314
  52.1 0.1 bitcast_reduce_fusion
  52.2 0.2 copy.24
  52.4 0.2 copy.25
  52.6 0.2 pad_maximum_fusion.q_ref
  52.8 0.1 copy.21
  52.9 8.2 %fusion.2 = bf16[8,128,2048]{2,1,0:T(8,128)(2,1)} fusion(bf16[1024,2048]{1,0:T(8,128)(2,1)} %x_ref.1, pred[8,1024]{1,0:T(8,128)(4,1)S(1)} %iota_compare_fusion, bf16[1024,128]{0,1:T(8,128)(2,1)S(1)} %copy.21), kind=kOutput, calls=%fused_computation.5 | convolution fusion | flops 4298113024 | bytes 8658944 | tf_op jit(solution)/shard_map/otr,td->ord/dot_general | solution.py:324
  61.2 0.0 copy-done.1
  61.2 73.7 %shard_map.96 = (bf16[8,2048,256]{2,1,0:T(8,128)(2,1)}, bf16[1024,2048]{1,0:T(8,128)(2,1)}) custom-call(bf16[2048,256]{1,0:T(8,128)(2,1)} %w_ref, bf16[1024,512]{1,0:T(8,128)(2,1)} %g_ref), custom_call_target="tpu_custom_call" | custom-call | tf_op jit(solution)/shard_map/pallas_call | solution.py:208
  134.9 0.0 all-to-all-done.1.a_ref
  134.9 7.7 %all-to-all-start.2 = ((bf16[8,128,2048]{2,1,0:T(8,128)(2,1)}), bf16[8,128,2048]{2,1,0:T(8,128)(2,1)}, u32[]{:S(2)}, u32[]{:S(2)}) async-start(bf16[8,128,2048]{2,1,0:T(8,128)(2,1)} %fusion.2), calls=%async_computation.2 | async-start | bytes 8388608 | tf_op jit(solution)/shard_map/all_to_all | solution.py:303
  142.6 0.0 copy-start.6
  142.6 0.0 copy-start.2
  142.6 0.0 all-gather.3.cloned.1.call-start
  142.7 8.1 %shard_map.98 = bf16[1024,128]{1,0:T(8,128)(2,1)} custom-call(s32[8]{0:T(128)} %copy-done.1, bf16[1024,2048]{1,0:T(8,128)(2,1)} %x_ref.1, bf16[8,2048,128]{2,1,0:T(8,128)(2,1)} %all-to-all-done.1.a_ref), custom_call_target="tpu_custom_call" | custom-call | tf_op jit(solution)/shard_map/pallas_call | solution.py:42
  150.7 0.0 all-gather.3.cloned.1.call-update
  150.8 0.0 copy-done.6
  150.8 0.1 fusion.18
  150.9 0.0 copy-done.2
  150.9 0.0 copy-start.3
  150.9 2.2 %copy-done.3 = bf16[1024,2048]{1,0:T(8,128)(2,1)S(1)} copy-done((bf16[1024,2048]{1,0:T(8,128)(2,1)S(1)}, bf16[1024,2048]{1,0:T(8,128)(2,1)}, u32[]{:S(2)}) %copy-start.3) | copy-done | bytes 4194328
  153.1 0.0 copy-start.5
  153.1 14.7 %shard_map.97 = bf16[1024,2048]{1,0:T(8,128)(2,1)} custom-call(s32[8]{0:T(128)S(1)} %copy-done.2, bf16[1024,2048]{1,0:T(8,128)(2,1)S(1)} %copy-done.3, bf16[8,2048,256]{2,1,0:T(8,128)(2,1)} %get-tuple-element.20.w_ref, bf16[8,2048,128]{2,1,0:T(8,128)(2,1)} %all-to-all-done.1.a_ref, bf16[1024,128]{1,0:T(8,128)(2,1)S(1)} %pad_maximum_fusion.q_ref), custom_call_target="tpu_custom_call" | custom-call | flops 9126805504 | bytes 16777216 | tf_op jit(solution)/shard_map/pallas_call | solution.py:248
  167.7 10.2 %all-gather.3.cloned.1.call-done = bf16[4096,128]{1,0:T(8,128)(2,1)} async-done(((bf16[1024,128]{1,0:T(8,128)(2,1)}), bf16[4096,128]{1,0:T(8,128)(2,1)}) %all-gather.3.cloned.1.call-update) | async-done | bytes 1048592 | tf_op jit(solution)/shard_map/all_gather | solution.py:335
  177.9 1.6 dynamic-slice_reduce_fusion
  179.6 0.1 copy.22
  179.7 0.0 copy-done.5
  179.7 1.5 convolution_convert_fusion
  181.2 11.1 %all-to-all-done.2 = bf16[8,128,2048]{2,1,0:T(8,128)(2,1)} async-done(((bf16[8,128,2048]{2,1,0:T(8,128)(2,1)}), bf16[8,128,2048]{2,1,0:T(8,128)(2,1)}, u32[]{:S(2)}, u32[]{:S(2)}) %all-to-all-start.2) | async-done | bytes 4194336 | tf_op jit(solution)/shard_map/all_to_all | solution.py:303
  192.3 3.7 %all-to-all-start.3 = ((bf16[8,64,512]{2,1,0:T(8,128)(2,1)}), bf16[8,64,512]{2,1,0:T(8,128)(2,1)S(1)}, u32[]{:S(2)}, u32[]{:S(2)}) async-start(bf16[8,64,512]{2,1,0:T(8,128)(2,1)} %convolution_convert_fusion), calls=%async_computation.3 | async-start | bytes 1048576 | tf_op jit(solution)/shard_map/all_to_all | solution.py:303
  196.0 7.1 %select_reduce_fusion = bf16[4,128,2048]{2,1,0:T(8,128)(2,1)S(1)} fusion(pred[8,4]{1,0:T(8,128)(4,1)S(1)} %fusion.18, bf16[8,128,2048]{2,1,0:T(8,128)(2,1)} %all-to-all-done.2), kind=kLoop, calls=%fused_computation.2 | loop fusion | flops 15728640 | bytes 6291488 | tf_op jit(solution)/shard_map/reduce_sum | solution.py:348
  203.1 2.5 %copy.23 = bf16[4,2048,128]{2,1,0:T(8,128)(2,1)} copy(bf16[4,2048,128]{1,2,0:T(8,128)(2,1)S(1)} %bitcast.29) | data formatting | bytes 4194304
  205.5 0.0 all-to-all-done.3
  205.5 1.1 select_reduce_fusion.1
  (6 shorter events, 0.1 us)
Async XLA Ops:
  7.2 0.7 copy-start
  14.6 15.2 %all-to-all-start = ((bf16[8,64,512]{2,1,0:T(8,128)(2,1)}), bf16[8,64,512]{2,1,0:T(8,128)(2,1)S(1)}, u32[]{:S(2)}, u32[]{:S(2)}) async-start(bf16[8,64,512]{2,1,0:T(8,128)(2,1)} %shard_map.94), calls=%async_computation | async-start | bytes 1048576 | tf_op jit(solution)/shard_map/all_to_all | solution.py:303
  26.8 8.3 %copy-start.4 = (bf16[1024,512]{1,0:T(8,128)(2,1)S(1)}, bf16[1024,512]{1,0:T(8,128)(2,1)}, u32[]{:S(2)}) copy-start(bf16[1024,512]{1,0:T(8,128)(2,1)} %g_ref) | copy-start | bytes 3145732
  29.8 105.1 %all-to-all-start.1 = ((bf16[8,2048,128]{2,1,0:T(8,128)(2,1)}), bf16[8,2048,128]{2,1,0:T(8,128)(2,1)}, u32[]{:S(2)}, u32[]{:S(2)}) async-start(bf16[8,2048,128]{2,1,0:T(8,128)(2,1)} %shard_map.95), calls=%async_computation.1 | async-start | bytes 8388608 | tf_op jit(solution)/shard_map/all_to_all | solution.py:303
  34.4 26.8 %copy-start.1 = (s32[8]{0:T(128)}, s32[8]{0:T(128)S(1)}, u32[]{:S(2)}) copy-start(s32[8]{0:T(128)S(1)} %fusion.21.index_ref) | copy-start | bytes 100
  134.9 57.4 %all-to-all-start.2 = ((bf16[8,128,2048]{2,1,0:T(8,128)(2,1)}), bf16[8,128,2048]{2,1,0:T(8,128)(2,1)}, u32[]{:S(2)}, u32[]{:S(2)}) async-start(bf16[8,128,2048]{2,1,0:T(8,128)(2,1)} %fusion.2), calls=%async_computation.2 | async-start | bytes 8388608 | tf_op jit(solution)/shard_map/all_to_all | solution.py:303
  142.6 8.2 %copy-start.6 = (s32[8]{0:T(128)S(1)}, s32[8]{0:T(128)}, u32[]{:S(2)}) copy-start(s32[8]{0:T(128)} %fusion.16.index_ref) | copy-start | bytes 100
  142.6 8.3 %copy-start.2 = (s32[8]{0:T(128)S(1)}, s32[8]{0:T(128)}, u32[]{:S(2)}) copy-start(s32[8]{0:T(128)} %copy-done.1) | copy-start | bytes 100
  142.6 35.3 %all-gather.3.cloned.1.call-start = ((), (), s32[]{:S(2)}) async-start(), calls=%async_computation.4 | async-start | bytes 1310720 | tf_op jit(solution)/shard_map/all_gather | solution.py:335
  150.9 2.2 %copy-start.3 = (bf16[1024,2048]{1,0:T(8,128)(2,1)S(1)}, bf16[1024,2048]{1,0:T(8,128)(2,1)}, u32[]{:S(2)}) copy-start(bf16[1024,2048]{1,0:T(8,128)(2,1)} %get-tuple-element.17.g_ref) | copy-start | bytes 12582916
  153.1 26.7 %copy-start.5 = (bf16[1024,512]{1,0:T(8,128)(2,1)S(1)}, bf16[1024,512]{1,0:T(8,128)(2,1)}, u32[]{:S(2)}) copy-start(bf16[1024,512]{1,0:T(8,128)(2,1)} %g_ref) | copy-start | bytes 3145732
  192.3 13.2 %all-to-all-start.3 = ((bf16[8,64,512]{2,1,0:T(8,128)(2,1)}), bf16[8,64,512]{2,1,0:T(8,128)(2,1)S(1)}, u32[]{:S(2)}, u32[]{:S(2)}) async-start(bf16[8,64,512]{2,1,0:T(8,128)(2,1)} %convolution_convert_fusion), calls=%async_computation.3 | async-start | bytes 1048576 | tf_op jit(solution)/shard_map/all_to_all | solution.py:303
Sparse Core Ops, SparseCore 0:
  150.9 27.0 all-gather.2

commit v3 on v2

--- a/solution.py
+++ b/solution.py
@@ -10,24 +10,6 @@
 KEY_VALUE_WIDTH = 1024
 BLOCK = 128
 MESH = pl.DeviceIdType.MESH
-
-
-def copy_body(index_ref, from_ref, to_ref):
-    to_ref[...] = from_ref[...]
-
-
-def pick_rows(index, stacked):
-    shape = (1,) + stacked.shape[1:]
-    return pl.pallas_call(
-        copy_body,
-        grid_spec=pltpu.PrefetchScalarGridSpec(
-            num_scalar_prefetch=1,
-            grid=(index.shape[0],),
-            in_specs=[pl.BlockSpec(shape, lambda k, index_ref: (index_ref[k], 0, 0))],
-            out_specs=pl.BlockSpec(shape, lambda k, index_ref: (k, 0, 0)),
-        ),
-        out_shape=jax.ShapeDtypeStruct(index.shape + stacked.shape[1:], stacked.dtype),
-    )(index, stacked)
 
 
 def inner_body(index_ref, x_ref, a_ref, out_ref):
@@ -54,9 +36,16 @@
     )(index, tokens, maps)
 
 
-def gather_body(chips, ring, w_ref, g_ref, w_out, g_out, w_send, w_recv, f_send, f_recv, g_send, g_recv, here):
+def gather_body(
+    chips, ring, wanted_ref, owner_ref, w_ref, g_ref, down_ref, up_ref,
+    w_out, g_out, a_out, q_out,
+    out_a, out_b, in_b, q_box,
+    w_send, w_recv, f_send, f_recv, g_send, g_recv,
+    a_send, a_recv, b_send, b_recv, q_send, q_recv, here,
+):
     own = lax.axis_index("own")
     fsdp = lax.axis_index("fsdp")
+    count = 2 * chips
     chip, core = own // 2, lax.rem(own, 2)
     sibling = chip * 2 + 1 - core
     columns = g_ref.shape[1]
@@ -72,23 +61,56 @@
     keep_w.start()
     keep_g.start()
 
+    def peer(k):
+        return lax.rem(own + k, count)
+
+    def source(k):
+        return lax.rem(own + count - k, count)
+
     barrier = pltpu.get_barrier_semaphore()
-    for k in range(1, chips):
+    for k in range(1, count):
+        pl.semaphore_signal(barrier, inc=1, device_id={"own": peer(k)}, device_id_type=MESH)
+    for k in range(1, ring):
         pl.semaphore_signal(
-            barrier, inc=1, device_id={"own": chip_of(k) * 2 + core}, device_id_type=MESH
-        )
-    pl.semaphore_signal(barrier, inc=1, device_id={"own": sibling}, device_id_type=MESH)
-
-    @pl.when(fsdp > 0)
-    def _():
-        pl.semaphore_signal(barrier, inc=1, device_id={"fsdp": fsdp - 1}, device_id_type=MESH)
-
-    @pl.when(fsdp < ring - 1)
-    def _():
-        pl.semaphore_signal(barrier, inc=1, device_id={"fsdp": fsdp + 1}, device_id_type=MESH)
-
-    inside = (fsdp > 0).astype(jnp.int32) + (fsdp < ring - 1).astype(jnp.int32)
-    pl.semaphore_wait(barrier, chips + inside)
+            barrier, inc=1, device_id={"fsdp": lax.rem(fsdp + k, ring)}, device_id_type=MESH
+        )
+    for k in range(count):
+        out_b[k] = up_ref[wanted_ref[peer(k)]]
+    in_b[own] = out_b[0]
+    pl.semaphore_wait(barrier, count + ring - 2)
+
+    def b_copy(k, slot):
+        return pltpu.make_async_remote_copy(
+            src_ref=out_b.at[k],
+            dst_ref=in_b.at[slot],
+            send_sem=b_send.at[k - 1],
+            recv_sem=b_recv.at[k - 1],
+            device_id={"own": peer(k)},
+            device_id_type=MESH,
+        )
+
+    def a_copy(k, slot):
+        return pltpu.make_async_remote_copy(
+            src_ref=out_a.at[k],
+            dst_ref=a_out.at[slot],
+            send_sem=a_send.at[k - 1],
+            recv_sem=a_recv.at[k - 1],
+            device_id={"own": peer(k)},
+            device_id_type=MESH,
+        )
+
+    def q_copy(k, slot):
+        return pltpu.make_async_remote_copy(
+            src_ref=q_box.at[fsdp],
+            dst_ref=q_box.at[slot],
+            send_sem=q_send.at[k - 1],
+            recv_sem=q_recv.at[k - 1],
+            device_id={"fsdp": lax.rem(fsdp + k, ring)},
+            device_id_type=MESH,
+        )
+
+    for k in range(1, count):
+        b_copy(k, own).start()
 
     def g_copy(way, k):
         sign = 1 if way == 0 else -1
@@ -154,6 +176,47 @@
     for k in range(1, chips):
         w_copy(k).start()
     w_forward(0).start()
+
+    for k in list(range(1, count)) + [0]:
+        out_a[k] = down_ref[wanted_ref[peer(k)]]
+        if k:
+            a_copy(k, own).start()
+    keep_a = pltpu.make_async_copy(out_a.at[0], a_out.at[own], here.at[2])
+    keep_a.start()
+
+    for k in range(1, count):
+        b_copy(k, source(k)).wait_recv()
+    rows = g_ref.shape[0]
+    half, rank = rows // 2, up_ref.shape[1]
+    parts = []
+    for j in range(rows // BLOCK):
+        parts.append(
+            lax.dot_general(
+                g_ref[j * BLOCK : (j + 1) * BLOCK, :],
+                in_b[owner_ref[j]],
+                (((1,), (1,)), ((), ())),
+                preferred_element_type=jnp.float32,
+            )
+        )
+    mid = len(parts) // 2
+    q_box[fsdp] = jnp.concatenate(
+        [jnp.concatenate(parts[:mid], axis=0), jnp.concatenate(parts[mid:], axis=0)], axis=1
+    ).astype(jnp.bfloat16)
+    for k in range(1, ring):
+        q_copy(k, fsdp).start()
+    for k in range(1, ring):
+        q_copy(k, lax.rem(fsdp + ring - k, ring)).wait_recv()
+    sums = []
+    for side in range(2):
+        total = q_box[side * (ring // 2)].astype(jnp.float32)
+        for f in range(1, ring // 2):
+            total = total + q_box[side * (ring // 2) + f].astype(jnp.float32)
+        sums.append(total)
+    for part in range(2):
+        lanes = slice(part * rank, (part + 1) * rank)
+        q_out[part * half : (part + 1) * half, :] = jnp.concatenate(
+            [sums[0][:, lanes], sums[1][:, lanes]], axis=1
+        ).astype(q_out.dtype)
 
     for k in range(max(ring - 1, chips - 1)):
         if k < ring - 1:
@@ -196,34 +259,60 @@
             @pl.when(g_sends(way, k))
             def _():
                 g_copy(way, k).wait_send()
+    for k in range(1, ring):
+        q_copy(k, fsdp).wait_send()
+    for k in range(1, count):
+        a_copy(k, source(k)).wait_recv()
+        a_copy(k, own).wait_send()
+        b_copy(k, own).wait_send()
     keep_w.wait()
     keep_g.wait()
-
-
-def gather(weight, cotangent):
+    keep_a.wait()
+
+
+def gather(wanted, owner, weight, cotangent, down, up):
     own_count, ring = lax.axis_size("own"), lax.axis_size("fsdp")
     chips = own_count // 2
+    rows, columns = cotangent.shape
+    rank = down.shape[2]
     hbm = pl.BlockSpec(memory_space=pl.ANY)
+    vmem = pl.BlockSpec(memory_space=pltpu.VMEM)
+    smem = pl.BlockSpec(memory_space=pltpu.SMEM)
     dma = pltpu.SemaphoreType.DMA
+    others = dma((own_count - 1,))
     return pl.pallas_call(
         functools.partial(gather_body, chips, ring),
         out_shape=(
             jax.ShapeDtypeStruct((own_count,) + weight.shape, weight.dtype),
-            jax.ShapeDtypeStruct((cotangent.shape[0], cotangent.shape[1] * ring), cotangent.dtype),
-        ),
-        in_specs=[hbm, hbm],
-        out_specs=(hbm, hbm),
+            jax.ShapeDtypeStruct((rows, columns * ring), cotangent.dtype),
+            jax.ShapeDtypeStruct((own_count,) + down.shape[1:], down.dtype),
+            jax.ShapeDtypeStruct((rows, rank), jnp.bfloat16),
+        ),
+        in_specs=[smem, smem, hbm, vmem, vmem, vmem],
+        out_specs=(hbm, hbm, hbm, vmem),
         scratch_shapes=[
+            pltpu.VMEM((own_count,) + down.shape[1:], down.dtype),
+            pltpu.VMEM((own_count,) + up.shape[1:], up.dtype),
+            pltpu.VMEM((own_count,) + up.shape[1:], up.dtype),
+            pltpu.VMEM((ring, rows // 2, rank), jnp.bfloat16),
             dma((chips - 1,)),
             dma((chips - 1,)),
             dma((chips,)),
             dma((chips,)),
             dma((2, ring - 1)),
             dma((2, ring - 1)),
-            dma((2,)),
+            others,
+            others,
+            others,
+            others,
+            dma((ring - 1,)),
+            dma((ring - 1,)),
+            dma((3,)),
         ],
-        compiler_params=pltpu.CompilerParams(collective_id=0, has_side_effects=True),
-    )(weight, cotangent)
+        compiler_params=pltpu.CompilerParams(
+            collective_id=0, has_side_effects=True, vmem_limit_bytes=32 * 1024 * 1024
+        ),
+    )(wanted, owner, weight, cotangent, down, up)
 
 
 def grad_body(index_ref, g_ref, w_ref, a_ref, q_ref, out_ref, total):
@@ -267,6 +356,31 @@
             transcendentals=0,
         ),
     )(index, cotangent, weight, maps, q_low)
+
+
+def sum_body(mask_ref, back_ref, out_ref):
+    count, held = back_ref.shape[0], out_ref.shape[0]
+    for s in range(held):
+        total = jnp.zeros(back_ref.shape[1:], jnp.float32)
+        for b in range(count):
+            term = back_ref[b].astype(jnp.float32)
+            total = total + jnp.where(mask_ref[b * held + s] != 0, term, 0.0)
+        out_ref[s] = total.T.astype(out_ref.dtype)
+
+
+def sum_served(mask, back, held):
+    count, rank, width = back.shape
+    tile = 256
+    return pl.pallas_call(
+        sum_body,
+        grid_spec=pltpu.PrefetchScalarGridSpec(
+            num_scalar_prefetch=1,
+            grid=(width // tile,),
+            in_specs=[pl.BlockSpec((count, rank, tile), lambda k, mask_ref: (0, 0, k))],
+            out_specs=pl.BlockSpec((held, tile, rank), lambda k, mask_ref: (0, k, 0)),
+        ),
+        out_shape=jax.ShapeDtypeStruct((held, width, rank), back.dtype),
+    )(mask, back)
 
 
 def after(value, *others):
@@ -302,33 +416,14 @@
     def exchange(value):
         return lax.all_to_all(value, "own", split_axis=0, concat_axis=0, tiled=True)
 
-    fetched_b = exchange(pick_rows(wanted_local, up_weight))
-    outgoing_down = after(pick_rows(wanted_local, down_weight), fetched_b)
-    fetched_a = exchange(outgoing_down)
-
-    g_blocks = cotangent.reshape(block_count, BLOCK, col_count)
-    block_b = fetched_b[my_owner]
-    q_single = jnp.einsum(
-        "btc,brc->btr", g_blocks, block_b, preferred_element_type=jnp.float32
-    ).reshape(tok_rows, rank_half)
-    q_all = lax.all_gather(q_single.astype(jnp.bfloat16), "fsdp", axis=0)
-    q_low = (
-        q_all.reshape(2, fsdp_count // 2, tok_rows, rank_half)
-        .astype(jnp.float32)
-        .sum(axis=1)
-        .astype(jnp.bfloat16)
+    weight_rows, full_grad, fetched_a, q_low = gather(
+        wanted_local, my_owner, frozen_weight, cotangent, down_weight, up_weight
     )
-    q_low = jnp.concatenate([q_low[0], q_low[1]], axis=1)
     q_wide = jnp.where(row_mask[:, :, None], q_low[None], jnp.bfloat16(0))
 
     part_a = jnp.einsum(
         "otr,td->ord", q_wide, activations, preferred_element_type=jnp.float32
     ).astype(jnp.bfloat16)
-    late_weight, late_cotangent, part_a, outgoing_down = lax.optimization_barrier(
-        (frozen_weight, cotangent, part_a, outgoing_down)
-    )
-    weight_rows, full_grad = gather(late_weight, late_cotangent)
-    fetched_a, part_a, weight_rows = lax.optimization_barrier((fetched_a, part_a, weight_rows))
     back_a = exchange(part_a)
 
     inner_part = inner_product(my_owner, activations, fetched_a)
@@ -347,7 +442,11 @@
         terms = jnp.where(serve_mask[:, :, None, None], back[:, None], jnp.bfloat16(0))
         return terms.astype(jnp.float32).sum(axis=0).astype(jnp.bfloat16)
 
-    down_gradient = accumulate(after(back_a, activation_gradient)).transpose(0, 2, 1)
+    down_gradient = sum_served(
+        serve_mask.astype(jnp.int32).reshape(-1),
+        after(back_a, activation_gradient),
+        resident_count,
+    )
     back_b = exchange(after(part_b, back_a))
     up_gradient = accumulate(back_b)
     return (activation_gradient, down_gradient, up_gradient)

time: 215 us -> 225 us (1.047)
  Pallas kernels: 108 us -> 133 us
  blocking collectives: 16.4 us -> 0 us
  starting transfers between devices: 21.4 us -> 8.1 us
  waiting for transfers between devices: 24.3 us -> 37 us
  local copies, waits for them, and re-layouts: 7.04 us -> 18.4 us
  other arithmetic: 11.6 us -> 3.71 us
    pallas_call x1, Pallas kernels: 73.7 us -> 102 us  [gather(): pl.pallas_call(functools.partial(gather_body, chips, ring), out_shape=(ja...]
    all_gather x1, waiting for transfers between devices: 10.2 us -> 28.5 us  [shards(): inner_all = lax.all_gather(inner_part, 'fsdp', axis=0)]
    all_gather x1 -> x0, blocking collectives: 16.4 us -> none  [shards(): q_all = lax.all_gather(q_single.astype(jnp.bfloat16), 'fsdp', axis=0)]
    all_to_all x4 -> x2, starting transfers between devices: 21.4 us -> 8.06 us  [exchange(): return lax.all_to_all(value, 'own', split_axis=0, concat_axis=0, tiled=True)]
    unnamed x17 -> x26, local copies, waits for them, and re-layouts: 5.07 us -> 16.6 us
    reduce_sum x2 -> x1, other arithmetic: 8.13 us -> 1.06 us  [accumulate(): return terms.astype(jnp.float32).sum(axis=0).astype(jnp.bfloat16)]
    all_to_all x4 -> x2, waiting for transfers between devices: 14 us -> 8.47 us  [exchange(): return lax.all_to_all(value, 'own', split_axis=0, concat_axis=0, tiled=True)]
    pallas_call x2 -> x1, Pallas kernels: 11.9 us -> 8.23 us  [sum_served(): pl.pallas_call(sum_body, grid_spec=pltpu.PrefetchScalarGridSpec(num_scala...]
  transfers between devices with their start and end apart: 5 -> 3, of which waited for: 3 -> 2; matrix products, arithmetic and copies ran while one was open for 11% -> 2% of each run, Pallas kernels for 48% -> 14%
where the time goes in v3:
time: 225 us; the launch traced here: 224 us
  Pallas kernels  133 us (59%)
  waiting for transfers between devices  37 us (16%)
  local copies, waits for them, and re-layouts  18.4 us (8%)
  between operations  14.2 us (6%)
  matrix products  9.75 us (4%)
  starting transfers between devices  8.1 us (4%)
  other arithmetic  3.71 us (2%)
    pallas_call x1, Pallas kernels, gather(): pl.pallas_call(functools.partial(gather_body, chips, ring), out_shape=(ja...  102 us
    all_gather x1, waiting for transfers between devices, shards(): inner_all = lax.all_gather(inner_part, 'fsdp', axis=0)  28.5 us
    unnamed x26, local copies, waits for them, and re-layouts  16.6 us
    pallas_call x1, Pallas kernels, activation_grad(): pl.pallas_call(grad_body, grid_spec=pltpu.PrefetchScalarGridSpec(num_scal...  14.4 us
    all_to_all x2, waiting for transfers between devices, exchange(): return lax.all_to_all(value, 'own', split_axis=0, concat_axis=0, tiled=True)  8.47 us
    dot_general x1, matrix products, shards(): jnp.einsum('otr,td->ord', q_wide, activations, preferred_element_type=jnp...  8.24 us
    pallas_call x1, Pallas kernels, sum_served(): pl.pallas_call(sum_body, grid_spec=pltpu.PrefetchScalarGridSpec(num_scala...  8.23 us
    pallas_call x1, Pallas kernels, inner_product(): pl.pallas_call(inner_body, grid_spec=pltpu.PrefetchScalarGridSpec(num_sca...  8.2 us
  transfers between devices with their start and end apart: 3, of which 2 were waited for; matrix products, arithmetic and copies ran while one was open for 2% of the time, Pallas kernels for 14%

profile of v3, /device:TPU:0, one launch (start us, length us, event | category | flops | bytes accessed | tf_op | source)
XLA Modules:
  0.0 223.9 jit_solution(10414187484614900274)
XLA Ops:
  7.2 0.0 copy-start
  7.2 0.7 compare_select_fusion
  7.9 0.0 copy-done
  7.9 0.8 gather_fusion
  8.6 0.1 reshape.76
  8.7 0.1 fusion.22
  8.8 0.1 fusion.15.wanted_ref
  9.0 0.0 copy-start.8
  9.0 0.1 broadcast_bitcast_fusion
  9.1 0.0 copy-start.3
  9.1 1.6 copy-done.3
  10.7 0.0 copy-start.4
  10.7 1.2 copy-done.4
  11.9 0.0 copy-start.5
  11.9 1.2 copy-done.5
  13.1 0.0 copy-start.7
  13.1 0.9 copy-done.7
  14.1 101.9 %shard_map.94 = (bf16[8,2048,256]{2,1,0:T(8,128)(2,1)S(1)}, bf16[1024,2048]{1,0:T(8,128)(2,1)S(1)}, bf16[8,2048,128]{2,1,0:T(8,128)(2,1)S(1)}, bf16[1024,128]{1,0:T(8,128)(2,1)S(1)}) custom-call(s32[8]{0:T(128)S(1)} %fusion.15.wanted_ref, s32[8]{0:T(128)S(1)} %dynamic-slice_bitcast_fusion.owner_ref.index_ref, bf16[2048,256]{1,0:T(8,128)(2,1)S(1)} %copy-done.4, ...), custom_call_target="tpu_custom_call" | custom-call | tf_op jit(solution)/shard_map/pallas_call | solution.py:283
  116.0 0.0 copy-start.1
  116.0 2.0 copy-done.1
  118.0 0.0 copy-start.10
  118.0 3.2 %copy-done.10 = bf16[8,2048,256]{2,1,0:T(8,128)(2,1)} copy-done((bf16[8,2048,256]{2,1,0:T(8,128)(2,1)}, bf16[8,2048,256]{2,1,0:T(8,128)(2,1)S(1)}, u32[]{:S(2)}) %copy-start.10) | copy-done | bytes 8388632
  121.2 0.0 copy-start.11
  121.2 2.0 copy-done.11
  123.2 0.1 copy.14
  123.4 8.2 %fusion.2 = bf16[8,128,2048]{2,1,0:T(8,128)(2,1)} fusion(bf16[1024,2048]{1,0:T(8,128)(2,1)} %x_ref.1, pred[8,1024]{1,0:T(8,128)(4,1)S(1)} %iota_compare_fusion, bf16[1024,128]{0,1:T(8,128)(2,1)S(1)} %copy.14), kind=kOutput, calls=%fused_computation.3 | convolution fusion | flops 4298113024 | bytes 8658944 | tf_op jit(solution)/shard_map/otr,td->ord/dot_general | solution.py:424
  131.6 0.0 copy-done.8
  131.6 4.6 %all-to-all-start = ((bf16[8,128,2048]{2,1,0:T(8,128)(2,1)}), bf16[8,128,2048]{2,1,0:T(8,128)(2,1)}, u32[]{:S(2)}, u32[]{:S(2)}) async-start(bf16[8,128,2048]{2,1,0:T(8,128)(2,1)} %fusion.2), calls=%async_computation | async-start | bytes 8388608 | tf_op jit(solution)/shard_map/all_to_all | solution.py:417
  136.2 0.0 all-gather.3.cloned.1.call-start
  136.2 0.0 copy-start.6
  136.3 8.2 %shard_map.97 = bf16[1024,128]{1,0:T(8,128)(2,1)} custom-call(s32[8]{0:T(128)} %copy-done.8, bf16[1024,2048]{1,0:T(8,128)(2,1)} %x_ref.1, bf16[8,2048,128]{2,1,0:T(8,128)(2,1)} %copy-done.1), custom_call_target="tpu_custom_call" | custom-call | tf_op jit(solution)/shard_map/pallas_call | solution.py:24
  144.5 0.0 copy-start.9
  144.5 0.0 all-gather.3.cloned.1.call-update
  144.5 0.1 fusion.17
  144.6 0.6 reshape.77.mask_ref
  145.2 28.5 %all-gather.3.cloned.1.call-done = bf16[4096,128]{1,0:T(8,128)(2,1)} async-done(((bf16[1024,128]{1,0:T(8,128)(2,1)}), bf16[4096,128]{1,0:T(8,128)(2,1)}) %all-gather.3.cloned.1.call-update) | async-done | bytes 1048592 | tf_op jit(solution)/shard_map/all_gather | solution.py:430
  173.7 1.6 dynamic-slice_reduce_fusion
  175.3 0.1 copy.15
  175.4 0.0 copy-done.6
  175.4 1.5 convolution_convert_fusion
  177.0 8.5 %all-to-all-done.back_ref = bf16[8,128,2048]{2,1,0:T(8,128)(2,1)} async-done(((bf16[8,128,2048]{2,1,0:T(8,128)(2,1)}), bf16[8,128,2048]{2,1,0:T(8,128)(2,1)}, u32[]{:S(2)}, u32[]{:S(2)}) %all-to-all-start) | async-done | bytes 4194336 | tf_op jit(solution)/shard_map/all_to_all | solution.py:417
  185.4 3.5 %all-to-all-start.1 = ((bf16[8,64,512]{2,1,0:T(8,128)(2,1)}), bf16[8,64,512]{2,1,0:T(8,128)(2,1)S(1)}, u32[]{:S(2)}, u32[]{:S(2)}) async-start(bf16[8,64,512]{2,1,0:T(8,128)(2,1)} %convolution_convert_fusion), calls=%async_computation.1 | async-start | bytes 1048576 | tf_op jit(solution)/shard_map/all_to_all | solution.py:417
  188.9 0.0 copy-done.9
  188.9 0.0 copy-start.2
  188.9 2.2 copy-done.2
  191.1 0.0 copy-start.12
  191.1 2.2 copy-done.12
  193.3 14.4 %shard_map.95 = bf16[1024,2048]{1,0:T(8,128)(2,1)} custom-call(s32[8]{0:T(128)S(1)} %copy-done.9, bf16[1024,2048]{1,0:T(8,128)(2,1)S(1)} %copy-done.12, bf16[8,2048,256]{2,1,0:T(8,128)(2,1)} %copy-done.10, bf16[8,2048,128]{2,1,0:T(8,128)(2,1)S(1)} %copy-done.2, bf16[1024,128]{1,0:T(8,128)(2,1)S(1)} %get-tuple-element.12.q_ref), custom_call_target="tpu_custom_call" | custom-call | flops 9126805504 | bytes 16777216 | tf_op jit(solution)/shard_map/pallas_call | solution.py:337
  207.7 8.2 %shard_map.96 = bf16[4,2048,128]{2,1,0:T(8,128)(2,1)} custom-call(s32[32]{0:T(128)} %reshape.77.mask_ref, bf16[8,128,2048]{2,1,0:T(8,128)(2,1)} %all-to-all-done.back_ref), custom_call_target="tpu_custom_call" | custom-call | tf_op jit(solution)/shard_map/pallas_call | solution.py:374
  215.9 0.0 all-to-all-done.1
  215.9 1.1 select_reduce_fusion
  (3 shorter events, 0.0 us)
Async XLA Ops:
  7.2 0.7 copy-start
  9.0 122.6 %copy-start.8 = (s32[8]{0:T(128)}, s32[8]{0:T(128)S(1)}, u32[]{:S(2)}) copy-start(s32[8]{0:T(128)S(1)} %dynamic-slice_bitcast_fusion.owner_ref.index_ref) | copy-start | bytes 100
  9.1 1.6 copy-start.3
  10.7 1.2 copy-start.4
  11.9 1.2 copy-start.5
  13.1 0.9 copy-start.7
  116.0 2.0 copy-start.1
  118.0 3.2 %copy-start.10 = (bf16[8,2048,256]{2,1,0:T(8,128)(2,1)}, bf16[8,2048,256]{2,1,0:T(8,128)(2,1)S(1)}, u32[]{:S(2)}) copy-start(bf16[8,2048,256]{2,1,0:T(8,128)(2,1)S(1)} %get-tuple-element.10.w_ref) | copy-start | bytes 25165828
  121.2 2.0 copy-start.11
  131.6 53.8 %all-to-all-start = ((bf16[8,128,2048]{2,1,0:T(8,128)(2,1)}), bf16[8,128,2048]{2,1,0:T(8,128)(2,1)}, u32[]{:S(2)}, u32[]{:S(2)}) async-start(bf16[8,128,2048]{2,1,0:T(8,128)(2,1)} %fusion.2), calls=%async_computation | async-start | bytes 8388608 | tf_op jit(solution)/shard_map/all_to_all | solution.py:417
  136.2 37.5 %all-gather.3.cloned.1.call-start = ((), (), s32[]{:S(2)}) async-start(), calls=%async_computation.2 | async-start | bytes 1310720 | tf_op jit(solution)/shard_map/all_gather | solution.py:430
  136.2 39.2 %copy-start.6 = (bf16[1024,512]{1,0:T(8,128)(2,1)S(1)}, bf16[1024,512]{1,0:T(8,128)(2,1)}, u32[]{:S(2)}) copy-start(bf16[1024,512]{1,0:T(8,128)(2,1)} %g_ref.1) | copy-start | bytes 3145732
  144.5 44.5 %copy-start.9 = (s32[8]{0:T(128)S(1)}, s32[8]{0:T(128)}, u32[]{:S(2)}) copy-start(s32[8]{0:T(128)} %copy-done.8) | copy-start | bytes 100
  185.4 30.5 %all-to-all-start.1 = ((bf16[8,64,512]{2,1,0:T(8,128)(2,1)}), bf16[8,64,512]{2,1,0:T(8,128)(2,1)S(1)}, u32[]{:S(2)}, u32[]{:S(2)}) async-start(bf16[8,64,512]{2,1,0:T(8,128)(2,1)} %convolution_convert_fusion), calls=%async_computation.1 | async-start | bytes 1048576 | tf_op jit(solution)/shard_map/all_to_all | solution.py:417
  188.9 2.2 copy-start.2
  191.1 2.2 copy-start.12
Sparse Core Ops, SparseCore 0:
  144.6 29.0 all-gather.2

commit v4 on v3

--- a/solution.py
+++ b/solution.py
@@ -37,9 +37,9 @@
 
 
 def gather_body(
-    chips, ring, wanted_ref, owner_ref, w_ref, g_ref, down_ref, up_ref,
-    w_out, g_out, a_out, q_out,
-    out_a, out_b, in_b, q_box,
+    chips, ring, wanted_ref, owner_ref, w_ref, g_ref, down_ref, up_ref, x_ref, line_ref,
+    w_out, g_out, a_out, q_out, pa_out,
+    out_a, out_b, in_b, q_box, x_held, pa_held,
     w_send, w_recv, f_send, f_recv, g_send, g_recv,
     a_send, a_recv, b_send, b_recv, q_send, q_recv, here,
 ):
@@ -58,8 +58,11 @@
 
     keep_w = pltpu.make_async_copy(w_ref, w_out.at[own], here.at[0])
     keep_g = pltpu.make_async_copy(g_ref, g_slice(fsdp), here.at[1])
+    keep_x = pltpu.make_async_copy(x_ref, x_held, here.at[3])
+    keep_pa = pltpu.make_async_copy(pa_held, pa_out, here.at[4])
     keep_w.start()
     keep_g.start()
+    keep_x.start()
 
     def peer(k):
         return lax.rem(own + k, count)
@@ -241,6 +244,19 @@
             ).wait_recv()
             w_forward(k + 1).start()
 
+    keep_x.wait()
+    turned = q_out[...].astype(jnp.float32).T
+
+    def owner_step(o, carry):
+        picked = jnp.where(line_ref[...] == o, turned, 0.0).astype(jnp.bfloat16)
+        pa_held[o] = jnp.dot(
+            picked, x_held[...], preferred_element_type=jnp.float32
+        ).astype(pa_held.dtype)
+        return carry
+
+    lax.fori_loop(0, count, owner_step, 0)
+    keep_pa.start()
+
     for k in range(chips):
         piece = w_origin(k, 1 - core)
         pltpu.make_async_remote_copy(
@@ -268,9 +284,10 @@
     keep_w.wait()
     keep_g.wait()
     keep_a.wait()
-
-
-def gather(wanted, owner, weight, cotangent, down, up):
+    keep_pa.wait()
+
+
+def gather(wanted, owner, weight, cotangent, down, up, tokens, line):
     own_count, ring = lax.axis_size("own"), lax.axis_size("fsdp")
     chips = own_count // 2
     rows, columns = cotangent.shape
@@ -287,14 +304,17 @@
             jax.ShapeDtypeStruct((rows, columns * ring), cotangent.dtype),
             jax.ShapeDtypeStruct((own_count,) + down.shape[1:], down.dtype),
             jax.ShapeDtypeStruct((rows, rank), jnp.bfloat16),
-        ),
-        in_specs=[smem, smem, hbm, vmem, vmem, vmem],
-        out_specs=(hbm, hbm, hbm, vmem),
+            jax.ShapeDtypeStruct((own_count, rank, tokens.shape[1]), jnp.bfloat16),
+        ),
+        in_specs=[smem, smem, hbm, vmem, vmem, vmem, hbm, vmem],
+        out_specs=(hbm, hbm, hbm, vmem, hbm),
         scratch_shapes=[
             pltpu.VMEM((own_count,) + down.shape[1:], down.dtype),
             pltpu.VMEM((own_count,) + up.shape[1:], up.dtype),
             pltpu.VMEM((own_count,) + up.shape[1:], up.dtype),
             pltpu.VMEM((ring, rows // 2, rank), jnp.bfloat16),
+            pltpu.VMEM(tokens.shape, tokens.dtype),
+            pltpu.VMEM((own_count, rank, tokens.shape[1]), jnp.bfloat16),
             dma((chips - 1,)),
             dma((chips - 1,)),
             dma((chips,)),
@@ -307,12 +327,12 @@
             others,
             dma((ring - 1,)),
             dma((ring - 1,)),
-            dma((3,)),
+            dma((5,)),
         ],
         compiler_params=pltpu.CompilerParams(
-            collective_id=0, has_side_effects=True, vmem_limit_bytes=32 * 1024 * 1024
-        ),
-    )(wanted, owner, weight, cotangent, down, up)
+            collective_id=0, has_side_effects=True, vmem_limit_bytes=60 * 1024 * 1024
+        ),
+    )(wanted, owner, weight, cotangent, down, up, tokens, line)
 
 
 def grad_body(index_ref, g_ref, w_ref, a_ref, q_ref, out_ref, total):
@@ -416,18 +436,22 @@
     def exchange(value):
         return lax.all_to_all(value, "own", split_axis=0, concat_axis=0, tiled=True)
 
-    weight_rows, full_grad, fetched_a, q_low = gather(
-        wanted_local, my_owner, frozen_weight, cotangent, down_weight, up_weight
+    weight_rows, full_grad, fetched_a, q_low, part_a = gather(
+        wanted_local,
+        my_owner,
+        frozen_weight,
+        cotangent,
+        down_weight,
+        up_weight,
+        activations,
+        owner_rows[None, :],
     )
-    q_wide = jnp.where(row_mask[:, :, None], q_low[None], jnp.bfloat16(0))
-
-    part_a = jnp.einsum(
-        "otr,td->ord", q_wide, activations, preferred_element_type=jnp.float32
-    ).astype(jnp.bfloat16)
     back_a = exchange(part_a)
 
     inner_part = inner_product(my_owner, activations, fetched_a)
     inner_all = lax.all_gather(inner_part, "fsdp", axis=0)
+    activation_gradient = activation_grad(my_owner, full_grad, weight_rows, fetched_a, q_low)
+    inner_all = after(inner_all, activation_gradient)
     proj_index = fsdp_index * col_count // KEY_VALUE_WIDTH
     inner_mine = lax.dynamic_slice_in_dim(inner_all, proj_index * rank_half, rank_half, 2)
     inner_mine = inner_mine.astype(jnp.float32).sum(axis=0).astype(jnp.bfloat16)
@@ -436,15 +460,13 @@
         "otr,tc->orc", inner_wide, cotangent, preferred_element_type=jnp.float32
     ).astype(jnp.bfloat16)
 
-    activation_gradient = activation_grad(my_owner, full_grad, weight_rows, fetched_a, q_low)
-
     def accumulate(back):
         terms = jnp.where(serve_mask[:, :, None, None], back[:, None], jnp.bfloat16(0))
         return terms.astype(jnp.float32).sum(axis=0).astype(jnp.bfloat16)
 
     down_gradient = sum_served(
         serve_mask.astype(jnp.int32).reshape(-1),
-        after(back_a, activation_gradient),
+        back_a,
         resident_count,
     )
     back_b = exchange(after(part_b, back_a))

time: 225 us -> 190 us (0.84)
  waiting for transfers between devices: 37 us -> 19.5 us
  local copies, waits for them, and re-layouts: 18.4 us -> 6.71 us
  matrix products: 9.75 us -> 1.5 us
    all_gather x1, waiting for transfers between devices: 28.5 us -> 10.2 us  [shards(): inner_all = lax.all_gather(inner_part, 'fsdp', axis=0)]
    unnamed x26 -> x16, local copies, waits for them, and re-layouts: 16.6 us -> 4.4 us
    dot_general x1 -> x0, matrix products: 8.24 us -> none  [shards(): jnp.einsum('otr,td->ord', q_wide, activations, preferred_element_type=jnp...]
  transfers between devices with their start and end apart: 3 -> 3, of which waited for: 2 -> 3; matrix products, arithmetic and copies ran while one was open for 2% -> 2% of each run, Pallas kernels for 14% -> 16%
where the time goes in v4:
time: 190 us; the launch traced here: 189 us
  Pallas kernels  135 us (71%)
  waiting for transfers between devices  19.5 us (10%)
  between operations  14.2 us (7%)
  starting transfers between devices  8.13 us (4%)
  local copies, waits for them, and re-layouts  6.71 us (4%)
  other arithmetic  4.26 us (2%)
    pallas_call x1, Pallas kernels, gather(): pl.pallas_call(functools.partial(gather_body, chips, ring), out_shape=(ja...  104 us
    pallas_call x1, Pallas kernels, activation_grad(): pl.pallas_call(grad_body, grid_spec=pltpu.PrefetchScalarGridSpec(num_scal...  14.4 us
    all_gather x1, waiting for transfers between devices, shards(): inner_all = lax.all_gather(inner_part, 'fsdp', axis=0)  10.2 us
    all_to_all x2, waiting for transfers between devices, exchange(): return lax.all_to_all(value, 'own', split_axis=0, concat_axis=0, tiled=True)  9.27 us
    pallas_call x1, Pallas kernels, inner_product(): pl.pallas_call(inner_body, grid_spec=pltpu.PrefetchScalarGridSpec(num_sca...  8.27 us
    pallas_call x1, Pallas kernels, sum_served(): pl.pallas_call(sum_body, grid_spec=pltpu.PrefetchScalarGridSpec(num_scala...  8.23 us
    all_to_all x2, starting transfers between devices, exchange(): return lax.all_to_all(value, 'own', split_axis=0, concat_axis=0, tiled=True)  8.09 us
    unnamed x16, local copies, waits for them, and re-layouts  4.4 us
  transfers between devices with their start and end apart: 3, of which 3 were waited for; matrix products, arithmetic and copies ran while one was open for 2% of the time, Pallas kernels for 16%

profile of v4, /device:TPU:0, one launch (start us, length us, event | category | flops | bytes accessed | tf_op | source)
XLA Modules:
  0.0 189.0 jit_solution(2663491814174366042)
XLA Ops:
  7.2 0.0 copy-start
  7.2 0.7 compare_select_fusion
  7.9 0.0 copy-done
  7.9 0.8 gather_fusion
  8.6 0.1 reshape.75
  8.7 0.1 fusion.12
  8.8 0.7 fusion.6.wanted_ref
  9.5 0.0 copy-start.2
  9.5 0.7 broadcast_in_dim.57
  10.2 0.0 copy-done.2
  10.2 103.8 %shard_map.94 = (bf16[8,2048,256]{2,1,0:T(8,128)(2,1)}, bf16[1024,2048]{1,0:T(8,128)(2,1)}, bf16[8,2048,128]{2,1,0:T(8,128)(2,1)}, bf16[1024,128]{1,0:T(8,128)(2,1)}, bf16[8,128,2048]{2,1,0:T(8,128)(2,1)}) custom-call(s32[8]{0:T(128)} %fusion.6.wanted_ref, s32[8]{0:T(128)} %copy-done.2, bf16[2048,256]{1,0:T(8,128)(2,1)} %w_ref.1, bf16[1024,512]{1,0:T(8,128)(2,1)} %g_ref.1, ...), custom_call_target="tpu_custom_call" | custom-call | tf_op jit(solution)/shard_map/pallas_call | solution.py:300
  114.0 4.6 %all-to-all-start = ((bf16[8,128,2048]{2,1,0:T(8,128)(2,1)}), bf16[8,128,2048]{2,1,0:T(8,128)(2,1)}, u32[]{:S(2)}, u32[]{:S(2)}) async-start(bf16[8,128,2048]{2,1,0:T(8,128)(2,1)} %get-tuple-element.14), calls=%async_computation | async-start | bytes 8388608 | tf_op jit(solution)/shard_map/all_to_all | solution.py:437
  118.6 0.0 all-gather.3.cloned.1.call-start
  118.7 0.0 copy-start.3
  118.7 0.0 copy-start.5
  118.7 8.3 %shard_map.97 = bf16[1024,128]{1,0:T(8,128)(2,1)} custom-call(s32[8]{0:T(128)} %copy-done.2, bf16[1024,2048]{1,0:T(8,128)(2,1)} %x_ref.3, bf16[8,2048,128]{2,1,0:T(8,128)(2,1)} %get-tuple-element.12.a_ref), custom_call_target="tpu_custom_call" | custom-call | tf_op jit(solution)/shard_map/pallas_call | solution.py:24
  126.9 0.0 all-gather.3.cloned.1.call-update
  127.0 0.0 copy-done.3
  127.0 0.1 broadcast_bitcast_fusion
  127.1 0.0 copy-done.5
  127.1 0.0 copy-start.1
  127.1 2.2 %copy-done.1 = bf16[8,2048,128]{2,1,0:T(8,128)(2,1)S(1)} copy-done((bf16[8,2048,128]{2,1,0:T(8,128)(2,1)S(1)}, bf16[8,2048,128]{2,1,0:T(8,128)(2,1)}, u32[]{:S(2)}) %copy-start.1) | copy-done | bytes 4194328
  129.3 0.0 copy-start.4
  129.3 2.2 %copy-done.4 = bf16[1024,2048]{1,0:T(8,128)(2,1)S(1)} copy-done((bf16[1024,2048]{1,0:T(8,128)(2,1)S(1)}, bf16[1024,2048]{1,0:T(8,128)(2,1)}, u32[]{:S(2)}) %copy-start.4) | copy-done | bytes 4194328
  131.5 0.0 copy-start.6
  131.5 14.4 %shard_map.95 = bf16[1024,2048]{1,0:T(8,128)(2,1)} custom-call(s32[8]{0:T(128)S(1)} %copy-done.3, bf16[1024,2048]{1,0:T(8,128)(2,1)S(1)} %copy-done.4, bf16[8,2048,256]{2,1,0:T(8,128)(2,1)} %get-tuple-element.11.w_ref, bf16[8,2048,128]{2,1,0:T(8,128)(2,1)S(1)} %copy-done.1, bf16[1024,128]{1,0:T(8,128)(2,1)S(1)} %copy-done.5), custom_call_target="tpu_custom_call" | custom-call | flops 9126805504 | bytes 16777216 | tf_op jit(solution)/shard_map/pallas_call | solution.py:357
  145.9 0.0 copy-start.7
  145.9 10.2 %all-gather.3.cloned.1.call-done = bf16[4096,128]{1,0:T(8,128)(2,1)} async-done(((bf16[1024,128]{1,0:T(8,128)(2,1)}), bf16[4096,128]{1,0:T(8,128)(2,1)}) %all-gather.3.cloned.1.call-update) | async-done | bytes 1048592 | tf_op jit(solution)/shard_map/all_gather | solution.py:452
  156.1 1.6 dynamic-slice_reduce_fusion
  157.8 0.1 copy.11
  157.9 0.0 copy-done.6
  157.9 1.5 convolution_convert_fusion
  159.4 8.5 %all-to-all-done.back_ref = bf16[8,128,2048]{2,1,0:T(8,128)(2,1)} async-done(((bf16[8,128,2048]{2,1,0:T(8,128)(2,1)}), bf16[8,128,2048]{2,1,0:T(8,128)(2,1)}, u32[]{:S(2)}, u32[]{:S(2)}) %all-to-all-start) | async-done | bytes 4194336 | tf_op jit(solution)/shard_map/all_to_all | solution.py:437
  167.9 3.5 %all-to-all-start.1 = ((bf16[8,64,512]{2,1,0:T(8,128)(2,1)}), bf16[8,64,512]{2,1,0:T(8,128)(2,1)S(1)}, u32[]{:S(2)}, u32[]{:S(2)}) async-start(bf16[8,64,512]{2,1,0:T(8,128)(2,1)} %convolution_convert_fusion), calls=%async_computation.1 | async-start | bytes 1048576 | tf_op jit(solution)/shard_map/all_to_all | solution.py:437
  171.4 0.0 copy-done.7
  171.4 0.1 fusion.8
  171.5 0.6 reshape.76.mask_ref
  172.1 8.2 %shard_map.96 = bf16[4,2048,128]{2,1,0:T(8,128)(2,1)} custom-call(s32[32]{0:T(128)} %reshape.76.mask_ref, bf16[8,128,2048]{2,1,0:T(8,128)(2,1)} %all-to-all-done.back_ref), custom_call_target="tpu_custom_call" | custom-call | tf_op jit(solution)/shard_map/pallas_call | solution.py:394
  180.3 0.8 all-to-all-done.1
  181.1 1.1 select_reduce_fusion
  (3 shorter events, 0.0 us)
Async XLA Ops:
  7.2 0.7 copy-start
  9.5 0.7 copy-start.2
  114.0 53.9 %all-to-all-start = ((bf16[8,128,2048]{2,1,0:T(8,128)(2,1)}), bf16[8,128,2048]{2,1,0:T(8,128)(2,1)}, u32[]{:S(2)}, u32[]{:S(2)}) async-start(bf16[8,128,2048]{2,1,0:T(8,128)(2,1)} %get-tuple-element.14), calls=%async_computation | async-start | bytes 8388608 | tf_op jit(solution)/shard_map/all_to_all | solution.py:437
  118.6 37.5 %all-gather.3.cloned.1.call-start = ((), (), s32[]{:S(2)}) async-start(), calls=%async_computation.2 | async-start | bytes 1310720 | tf_op jit(solution)/shard_map/all_gather | solution.py:452
  118.7 8.3 %copy-start.3 = (s32[8]{0:T(128)S(1)}, s32[8]{0:T(128)}, u32[]{:S(2)}) copy-start(s32[8]{0:T(128)} %copy-done.2) | copy-start | bytes 100
  118.7 8.4 %copy-start.5 = (bf16[1024,128]{1,0:T(8,128)(2,1)S(1)}, bf16[1024,128]{1,0:T(8,128)(2,1)}, u32[]{:S(2)}) copy-start(bf16[1024,128]{1,0:T(8,128)(2,1)} %get-tuple-element.13.q_ref) | copy-start | bytes 786436
  127.1 2.2 %copy-start.1 = (bf16[8,2048,128]{2,1,0:T(8,128)(2,1)S(1)}, bf16[8,2048,128]{2,1,0:T(8,128)(2,1)}, u32[]{:S(2)}) copy-start(bf16[8,2048,128]{2,1,0:T(8,128)(2,1)} %get-tuple-element.12.a_ref) | copy-start | bytes 12582916
  129.3 2.2 %copy-start.4 = (bf16[1024,2048]{1,0:T(8,128)(2,1)S(1)}, bf16[1024,2048]{1,0:T(8,128)(2,1)}, u32[]{:S(2)}) copy-start(bf16[1024,2048]{1,0:T(8,128)(2,1)} %get-tuple-element.10.g_ref) | copy-start | bytes 12582916
  131.5 26.4 %copy-start.6 = (bf16[1024,512]{1,0:T(8,128)(2,1)S(1)}, bf16[1024,512]{1,0:T(8,128)(2,1)}, u32[]{:S(2)}) copy-start(bf16[1024,512]{1,0:T(8,128)(2,1)} %g_ref.1) | copy-start | bytes 3145732
  145.9 25.5 %copy-start.7 = (s32[8]{0:T(128)S(1)}, s32[8]{0:T(128)}, u32[]{:S(2)}) copy-start(s32[8]{0:T(128)} %fusion.6.wanted_ref) | copy-start | bytes 100
  167.9 13.2 %all-to-all-start.1 = ((bf16[8,64,512]{2,1,0:T(8,128)(2,1)}), bf16[8,64,512]{2,1,0:T(8,128)(2,1)S(1)}, u32[]{:S(2)}, u32[]{:S(2)}) async-start(bf16[8,64,512]{2,1,0:T(8,128)(2,1)} %convolution_convert_fusion), calls=%async_computation.1 | async-start | bytes 1048576 | tf_op jit(solution)/shard_map/all_to_all | solution.py:437
Sparse Core Ops, SparseCore 0:
  127.1 29.0 all-gather.2
